TPU v7x, 512 devices: a whole 4x8x8 slice. The times are simulated.
512 devices in a mesh: seq: 128 (over x, z, y_lo), chan: 4 (over y_hi, core).
Axes of the slice: x: 4, y: 8 (y_hi: 2, y_lo: 4; y = y_hi * 4 + y_lo), z: 8, core: 2. Of those that a mesh axis runs over, the one named last changes fastest.
Arguments:
- inputs: bfloat16 [512, 512, 1024], P('seq', None, 'chan'), may hold values from -33 to 33
- norm_gain: float32 [1024], P('chan'), may hold values from 0.1 to 1.9
- inner_factor: bfloat16 [512, 512], replicated, may hold values from -0.25 to 0.25
- outer_factor: bfloat16 [512, 512], replicated, may hold values from -0.25 to 0.25
- twiddle: float32 [512, 512], P('seq'), may hold values from 0.5 to 2
- channel_weight: bfloat16 [4, 256, 256], P('chan'), may hold values from -0.375 to 0.375
- cotangent: bfloat16 [512, 512, 1024], P('seq', None, 'chan'), may hold values from -6 to 6
Outputs:
- input_grad: bfloat16 [512, 512, 1024], P('seq', None, 'chan')
- weight_grad: float32 [4, 256, 256], P('chan')
All inputs are finite; a program needn't handle non-finite values.
Results may differ from a plain program's by a relative error of at most 0.0071.
Values may be sent and summed in bfloat16 or wider, within the bound.
No kernel may reach another device: no remote copies, remote signals or barrier semaphores. Data moves between devices by JAX's collectives and lax.ppermute only.
A program may use at most 64 MiB of HBM per device.

v0:
```python
import jax
import jax.numpy as jnp
from jax import lax
from jax.sharding import PartitionSpec as P

D = 1024


GELU_C = 0.7978845608028654
GELU_A = 0.044715


def gelu_value(v):
    return 0.5 * v * (1.0 + jnp.tanh(GELU_C * (v + GELU_A * v * v * v)))


def gelu_slope(v):
    t = jnp.tanh(GELU_C * (v + GELU_A * v * v * v))
    return 0.5 * (1.0 + t) + 0.5 * v * (1.0 - t * t) * GELU_C * (1.0 + 3.0 * GELU_A * v * v)


def channel_grads(mixed, cot_part, weight_local):
    shape = mixed.shape
    nblocks = weight_local.shape[0]
    width = weight_local.shape[1]
    mixed_wide = mixed.astype(jnp.float32).reshape(-1, nblocks, width)
    hidden = gelu_value(mixed_wide).astype(jnp.bfloat16)
    cot_flat = cot_part.reshape(-1, nblocks, width)
    hidden_grad = jnp.einsum(
        "pbm,bkm->pbk", cot_flat, weight_local, preferred_element_type=jnp.float32
    )
    weight_part = jnp.einsum("pbk,pbm->bkm", hidden, cot_flat, preferred_element_type=jnp.float32)
    mixed_grad = (hidden_grad * gelu_slope(mixed_wide)).astype(jnp.bfloat16)
    return (mixed_grad.reshape(shape), weight_part)


def on_device(inputs, norm_gain, inner_factor, outer_factor, twiddle, channel_weight, cotangent):
    x_wide = inputs.astype(jnp.float32)
    sq_sum = lax.psum(jnp.sum(x_wide * x_wide, axis=-1), "chan")
    inv_rms = lax.rsqrt(sq_sum / D + 1e-05)
    normed = (x_wide * inv_rms[..., None] * norm_gain).astype(jnp.bfloat16)
    inner_out = jnp.einsum("ji,rid->rjd", inner_factor, normed, preferred_element_type=jnp.float32)
    rotated = (twiddle[..., None] * inner_out).astype(jnp.bfloat16)
    mixed_cols = jnp.einsum(
        "ji,icd->jcd",
        outer_factor,
        lax.all_to_all(rotated, "seq", split_axis=1, concat_axis=0, tiled=True),
        preferred_element_type=jnp.float32,
    ).astype(jnp.bfloat16)
    mixed_rows = lax.all_to_all(mixed_cols, "seq", split_axis=0, concat_axis=1, tiled=True)
    grad_rows, weight_part = channel_grads(mixed_rows, cotangent, channel_weight)
    rotated_grad = jnp.einsum(
        "ji,jcd->icd",
        outer_factor,
        lax.all_to_all(grad_rows, "seq", split_axis=1, concat_axis=0, tiled=True),
        preferred_element_type=jnp.float32,
    ).astype(jnp.bfloat16)
    scaled = (
        twiddle[..., None]
        * lax.all_to_all(rotated_grad, "seq", split_axis=0, concat_axis=1, tiled=True).astype(
            jnp.float32
        )
    ).astype(jnp.bfloat16)
    normed_grad = jnp.einsum(
        "ji,rjd->rid", inner_factor, scaled, preferred_element_type=jnp.float32
    )
    projection = lax.psum(jnp.sum(normed_grad * norm_gain * x_wide, axis=-1), "chan")
    input_grad = (
        cotangent.astype(jnp.float32)
        + inv_rms[..., None] * norm_gain * normed_grad
        - x_wide * (inv_rms**3)[..., None] * projection[..., None] / D
    )
    weight_grad = lax.psum(weight_part, "seq")
    return (input_grad.astype(jnp.bfloat16), weight_grad)


def solution(mesh):
    in_specs = (
        P("seq", None, "chan"),
        P("chan"),
        P(),
        P(),
        P("seq", None),
        P("chan", None, None),
        P("seq", None, "chan"),
    )
    out_specs = (P("seq", None, "chan"), P("chan", None, None))
    return jax.shard_map(
        on_device, mesh=mesh, in_specs=in_specs, out_specs=out_specs, check_vma=False
    )
```

profile of v0, /device:TPU:8, one launch (start us, length us, event | category | flops | bytes accessed | tf_op | source)
XLA Modules:
  0.0 1447.5 jit_solution(15569378625318485745)
XLA Ops:
  9.0 14.4 psum.21
  23.4 1.7 fusion.22
  26.8 43.3 %all_to_all.54 = bf16[4,512,256]{2,0,1:T(4,128)(2,1)S(1)} all-to-all(bf16[4,512,256]{2,0,1:T(4,128)(2,1)S(1)} %copy.65), channel_id=1, replica_groups=mesh['seq'=128,'chan'=4] {'seq'}, dimensions={1} | all-to-all | bytes 2097152 | tf_op jit(solution)/shard_map/all_to_all | solution.py:47
  72.8 36.8 %all_to_all.55 = bf16[512,4,256]{2,1,0:T(4,128)(2,1)S(1)} all-to-all(bf16[512,4,256]{2,1,0:T(4,128)(2,1)} %copy.68), channel_id=1, replica_groups=mesh['seq'=128,'chan'=4] {'seq'}, dimensions={0} | all-to-all | bytes 2097152 | tf_op jit(solution)/shard_map/all_to_all | solution.py:50
  109.9 2.6 copy.70
  112.5 3.0 reshape.154
  115.5 2.9 copy.74
  118.5 4.4 fusion.1
  122.8 2.6 reshape.153
  125.5 3.8 copy.78
  129.3 37.0 %all_to_all.56 = bf16[4,512,256]{2,0,1:T(4,128)(2,1)S(1)} all-to-all(bf16[4,512,256]{2,0,1:T(4,128)(2,1)} %copy.78), channel_id=1, replica_groups=mesh['seq'=128,'chan'=4] {'seq'}, dimensions={1} | all-to-all | bytes 2097152 | tf_op jit(solution)/shard_map/all_to_all | solution.py:55
  168.4 2.4 copy.81
  170.8 7.6 all-to-all-start.3
  178.6 2.3 copy.62
  183.1 1.8 copy.84
  184.9 2.1 convert_element_type.130
  187.0 2.4 convolution_bitcast_fusion.1
  189.5 18.3 %all-to-all-done.3 = bf16[512,4,256]{2,1,0:T(4,128)(2,1)} async-done(((bf16[512,4,256]{2,1,0:T(4,128)(2,1)}), bf16[512,4,256]{2,1,0:T(4,128)(2,1)}, u32[]{:S(2)}, u32[]{:S(2)}) %all-to-all-start.3) | async-done | bytes 1048608 | tf_op jit(solution)/shard_map/all_to_all | solution.py:60
  207.7 1.8 convert_bitcast_fusion
  211.0 2.1 fusion.19
  213.1 10.3 psum.22
  223.4 3.3 fusion.18
  226.7 2.3 copy.85
  229.0 1210.0 %all-reduce.2.cloned.1.call-done = f32[1,256,256]{2,1,0:T(8,128)} async-done(((f32[1,256,256]{2,1,0:T(8,128)}), f32[1,256,256]{2,1,0:T(8,128)}) %all-reduce.2.cloned.1.call-update) | async-done | bytes 262160 | tf_op jit(solution)/shard_map/psum | solution.py:73
  (32 shorter events, 14.0 us)
Async XLA Ops:
  7.2 16.2 %copy-start = (bf16[512,512]{1,0:T(8,128)(2,1)S(1)}, bf16[512,512]{1,0:T(8,128)(2,1)}, u32[]{:S(2)}) copy-start(bf16[512,512]{1,0:T(8,128)(2,1)} %param.9) | copy-start | bytes 1572868
  7.2 16.2 %copy-start.3 = (f32[4,512]{1,0:T(4,128)S(1)}, f32[4,512]{1,0:T(4,128)}, u32[]{:S(2)}) copy-start(f32[4,512]{1,0:T(4,128)} %param.11) | copy-start | bytes 24580
  7.2 16.2 %copy-start.4 = (f32[256]{0:T(256)S(1)}, f32[256]{0:T(256)}, u32[]{:S(2)}) copy-start(f32[256]{0:T(256)} %param.8) | copy-start | bytes 3076
  26.8 43.7 %copy-start.5 = (bf16[512,512]{1,0:T(8,128)(2,1)S(1)}, bf16[512,512]{1,0:T(8,128)(2,1)}, u32[]{:S(2)}) copy-start(bf16[512,512]{1,0:T(8,128)(2,1)} %param.10) | copy-start | bytes 1572868
  115.5 2.9 copy-start.6
  170.8 36.9 %all-to-all-start.3 = ((bf16[512,4,256]{2,1,0:T(4,128)(2,1)}), bf16[512,4,256]{2,1,0:T(4,128)(2,1)}, u32[]{:S(2)}, u32[]{:S(2)}) async-start(bf16[512,4,256]{2,1,0:T(4,128)(2,1)} %copy.81), calls=%async_computation.3 | async-start | bytes 2097152 | tf_op jit(solution)/shard_map/all_to_all | solution.py:60
  178.4 1260.6 %all-reduce.2.cloned.1.call-start = ((), (), s32[]{:S(2)}) async-start(), calls=%async_computation.4 | async-start | bytes 524288 | tf_op jit(solution)/shard_map/psum | solution.py:73
  183.1 4.0 copy-start.1
  211.0 12.4 copy-start.2
Sparse Core Ops, SparseCore 0:
  189.6 1249.3 all-reduce.1
where the time goes:
time: 1450 us
  waiting for transfers between devices  1230 us (85%)
  blocking collectives  142 us (10%)
  local copies, waits for them, and re-layouts  34.1 us (2%)
    psum x1, waiting for transfers between devices, on_device(): weight_grad = lax.psum(weight_part, 'seq')  1210 us
    all_to_all x1, blocking collectives, on_device(): lax.all_to_all(rotated, 'seq', split_axis=1, concat_axis=0, tiled=True)  43.3 us
    all_to_all x1, blocking collectives, on_device(): lax.all_to_all(grad_rows, 'seq', split_axis=1, concat_axis=0, tiled=True)  37 us
    all_to_all x1, blocking collectives, on_device(): lax.all_to_all(mixed_cols, 'seq', split_axis=0, concat_axis=1, tiled=True)  36.8 us
  transfers between devices with their start and end apart: 2, of which 2 were waited for; matrix products, arithmetic and copies ran while one was open for 2% of the time, Pallas kernels for 0%

commit v1 on v0

v1 whole, which is shorter than its diff:
```python
import jax
import jax.numpy as jnp
from jax import lax
from jax.sharding import PartitionSpec as P

D = 1024


GELU_C = 0.7978845608028654
GELU_A = 0.044715


def gelu_value(v):
    return 0.5 * v * (1.0 + jnp.tanh(GELU_C * (v + GELU_A * v * v * v)))


def gelu_slope(v):
    t = jnp.tanh(GELU_C * (v + GELU_A * v * v * v))
    return 0.5 * (1.0 + t) + 0.5 * v * (1.0 - t * t) * GELU_C * (1.0 + 3.0 * GELU_A * v * v)


def exchange(v):
    return lax.all_to_all(v, "seq", split_axis=0, concat_axis=0, tiled=True)


def to_columns(v, seq):
    r, n2, d = v.shape
    v = v.reshape(r, n2 // seq, seq, d).transpose(2, 0, 1, 3)
    return exchange(v.reshape(seq, r, -1)).reshape(seq * r, n2 // seq, d)


def on_device(seq, inputs, norm_gain, inner_factor, outer_factor, twiddle, channel_weight, cotangent):
    rows, n2, width = inputs.shape
    nh = n2 // seq
    cot = to_columns(cotangent, seq)
    x_wide = inputs.astype(jnp.float32)
    sq_sum = lax.psum(jnp.sum(x_wide * x_wide, axis=-1), "chan")
    inv_rms = lax.rsqrt(sq_sum / D + 1e-05)
    normed = (x_wide * inv_rms[..., None] * norm_gain).astype(jnp.bfloat16)
    inner_out = jnp.einsum("ji,rid->rjd", inner_factor, normed, preferred_element_type=jnp.float32)
    rotated = (twiddle[..., None] * inner_out).astype(jnp.bfloat16)
    mixed = jnp.einsum(
        "ji,ihd->jhd", outer_factor, to_columns(rotated, seq), preferred_element_type=jnp.float32
    ).astype(jnp.bfloat16)
    mixed_wide = mixed.astype(jnp.float32)
    hidden = gelu_value(mixed_wide).astype(jnp.bfloat16)
    weight = channel_weight[0]
    hidden_grad = jnp.einsum("jhm,km->jhk", cot, weight, preferred_element_type=jnp.float32)
    weight_part = jnp.einsum("jhk,jhm->km", hidden, cot, preferred_element_type=jnp.float32)
    mixed_grad = (hidden_grad * gelu_slope(mixed_wide)).astype(jnp.bfloat16)
    rotated_grad = jnp.einsum(
        "ji,jhd->ihd", outer_factor, mixed_grad, preferred_element_type=jnp.float32
    ).astype(jnp.bfloat16)
    back = exchange(rotated_grad.reshape(seq, rows, nh * width))
    back = back.reshape(seq, rows, nh, width).transpose(1, 2, 0, 3).reshape(rows, n2, width)
    scaled = (twiddle[..., None] * back.astype(jnp.float32)).astype(jnp.bfloat16)
    normed_grad = jnp.einsum("ji,rjd->rid", inner_factor, scaled, preferred_element_type=jnp.float32)
    projection = lax.psum(jnp.sum(normed_grad * norm_gain * x_wide, axis=-1), "chan")
    input_grad = (
        cotangent.astype(jnp.float32)
        + inv_rms[..., None] * norm_gain * normed_grad
        - x_wide * (inv_rms**3)[..., None] * projection[..., None] / D
    )
    pieces = exchange(weight_part.reshape(seq, width // seq, width))
    share = jnp.sum(pieces, axis=0)
    whole = exchange(jnp.broadcast_to(share, (seq,) + share.shape))
    return (input_grad.astype(jnp.bfloat16), whole.reshape(1, width, width))


def solution(mesh):
    in_specs = (
        P("seq", None, "chan"),
        P("chan"),
        P(),
        P(),
        P("seq", None),
        P("chan", None, None),
        P("seq", None, "chan"),
    )
    out_specs = (P("seq", None, "chan"), P("chan", None, None))

    def run(*args):
        return on_device(mesh.shape["seq"], *args)

    return jax.shard_map(run, mesh=mesh, in_specs=in_specs, out_specs=out_specs, check_vma=False)
```

time: 1450 us -> 215 us (0.15)
  the two profiles are of different devices: /device:TPU:8 before, /device:TPU:1 now
where the time goes in v1:
time: 215 us
  waiting for transfers between devices  76.5 us (36%)
  blocking collectives  45.7 us (21%)
  starting transfers between devices  38.7 us (18%)
  local copies, waits for them, and re-layouts  34.1 us (16%)
  matrix products  15.1 us (7%)
  other arithmetic  3.68 us (2%)
    all_to_all x4, waiting for transfers between devices, exchange(): return lax.all_to_all(v, 'seq', split_axis=0, concat_axis=0, tiled=True)  76.5 us
    all_to_all x4, starting transfers between devices, exchange(): return lax.all_to_all(v, 'seq', split_axis=0, concat_axis=0, tiled=True)  38.7 us
    all_to_all x1, blocking collectives, exchange(): return lax.all_to_all(v, 'seq', split_axis=0, concat_axis=0, tiled=True)  18.6 us
    psum x1, blocking collectives, on_device(): sq_sum = lax.psum(jnp.sum(x_wide * x_wide, axis=-1), 'chan')  15.9 us
    psum x1, blocking collectives, on_device(): lax.psum(jnp.sum(normed_grad * norm_gain * x_wide, axis=-1), 'chan')  11.2 us
    convert_element_type x3, local copies, waits for them, and re-layouts, on_device(): back.astype(jnp.float32)  9.08 us
    reshape x4, local copies, waits for them, and re-layouts, to_columns(): return exchange(v.reshape(seq, r, -1)).reshape(seq * r, n2 // seq, d)  8.91 us
    unnamed x17, local copies, waits for them, and re-layouts  6.17 us
  transfers between devices with their start and end apart: 4, of which 4 were waited for; matrix products, arithmetic and copies ran while one was open for 11% of the time, Pallas kernels for 0%

profile of v1, /device:TPU:1, one launch (start us, length us, event | category | flops | bytes accessed | tf_op | source)
XLA Modules:
  0.0 214.6 jit_solution(24718894376435680)
XLA Ops:
  2.5 15.9 %psum.14 = f32[4,512]{1,0:T(4,128)S(1)} all-reduce(f32[4,512]{1,0:T(4,128)S(1)} %fusion.16), channel_id=1, replica_groups=mesh['seq'=128,'chan'=4] {'chan'}, use_global_device_ids=true, to_apply=%region_1.0 | all-reduce | flops 2048 | bytes 16384 | tf_op jit(solution)/shard_map/psum | solution.py:37
  20.4 2.8 %copy.62 = bf16[128,4,1024]{2,1,0:T(4,128)(2,1)} copy(bf16[128,4,1024]{0,2,1:T(8,128)(2,1)} %bitcast.109) | data formatting | bytes 2097152 | tf_op jit(solution)/shard_map/reshape | solution.py:29
  23.2 13.0 %all-to-all-start.1 = ((bf16[128,4,1024]{2,1,0:T(4,128)(2,1)}), bf16[128,4,1024]{2,1,0:T(4,128)(2,1)}, u32[]{:S(2)}, u32[]{:S(2)}) async-start(bf16[128,4,1024]{2,1,0:T(4,128)(2,1)} %copy.62), calls=%async_computation.1 | async-start | bytes 2097152 | tf_op jit(solution)/shard_map/all_to_all | solution.py:23
  37.5 2.7 %copy.59 = bf16[128,4,1024]{2,1,0:T(4,128)(2,1)} copy(bf16[128,4,1024]{0,2,1:T(8,128)(2,1)} %bitcast.110) | data formatting | bytes 2097152 | tf_op jit(solution)/shard_map/reshape | solution.py:29
  40.2 24.5 %all-to-all-done.1 = bf16[128,4,1024]{2,1,0:T(4,128)(2,1)} async-done(((bf16[128,4,1024]{2,1,0:T(4,128)(2,1)}), bf16[128,4,1024]{2,1,0:T(4,128)(2,1)}, u32[]{:S(2)}, u32[]{:S(2)}) %all-to-all-start.1) | async-done | bytes 1048608 | tf_op jit(solution)/shard_map/all_to_all | solution.py:23
  64.7 7.9 %all-to-all-start = ((bf16[128,4,1024]{2,1,0:T(4,128)(2,1)}), bf16[128,4,1024]{2,1,0:T(4,128)(2,1)S(1)}, u32[]{:S(2)}, u32[]{:S(2)}) async-start(bf16[128,4,1024]{2,1,0:T(4,128)(2,1)} %copy.59), calls=%async_computation | async-start | bytes 2097152 | tf_op jit(solution)/shard_map/all_to_all | solution.py:23
  72.6 2.2 %reshape.46 = bf16[512,4,256]{2,1,0:T(4,128)(2,1)} reshape(bf16[128,4,1024]{2,1,0:T(4,128)(2,1)} %all-to-all-done.1) | data formatting | bytes 2097152 | tf_op jit(solution)/shard_map/reshape | solution.py:29
  74.8 3.7 %fusion.3 = (bf16[256,4,512]{0,2,1:T(8,128)(2,1)}, bf16[4,256,512]{1,2,0:T(8,128)(2,1)}) fusion(bf16[512,4,256]{2,1,0:T(4,128)(2,1)} %reshape.46, bf16[512,512]{1,0:T(8,128)(2,1)S(1)} %copy-done), kind=kOutput, calls=%fused_computation.12 | convolution fusion | flops 542638080 | bytes 3670016 | tf_op jit(solution)/shard_map/ji,ihd->jhd/dot_general | solution.py:42
  78.5 2.6 %copy.68 = bf16[256,4,512]{2,1,0:T(4,128)(2,1)} copy(bf16[256,4,512]{0,2,1:T(8,128)(2,1)} %get-tuple-element.16) | data formatting | bytes 2097152 | tf_op jit(solution)/shard_map/convert_element_type | solution.py:46
  81.1 21.2 %all-to-all-done = bf16[128,4,1024]{2,1,0:T(4,128)(2,1)S(1)} async-done(((bf16[128,4,1024]{2,1,0:T(4,128)(2,1)}), bf16[128,4,1024]{2,1,0:T(4,128)(2,1)S(1)}, u32[]{:S(2)}, u32[]{:S(2)}) %all-to-all-start) | async-done | bytes 1048608 | tf_op jit(solution)/shard_map/all_to_all | solution.py:23
  103.5 2.4 %convolution_bitcast_fusion = f32[128,2,256]{2,0,1:T(8,128)S(1)} fusion(bf16[128,2,4,512]{3,2,1,0:T(4,128)(2,1)} %bitcast.111, bf16[512,4,256]{2,1,0:T(4,128)(2,1)} %reshape.43), kind=kOutput, calls=%fused_computation.43 | convolution fusion | flops 268435456 | bytes 2359296 | tf_op jit(solution)/shard_map/jhk,jhm->km/dot_general | solution.py:49
  106.1 18.6 %all_to_all.25 = f32[128,2,256]{2,1,0:T(2,128)S(1)} all-to-all(f32[128,2,256]{2,1,0:T(2,128)S(1)} %copy.71), channel_id=1, replica_groups=mesh['seq'=128,'chan'=4] {'seq'}, dimensions={0} | all-to-all | bytes 524288 | tf_op jit(solution)/shard_map/all_to_all | solution.py:23
  125.7 8.6 %all-to-all-start.4 = ((f32[128,2,256]{2,1,0:T(2,128)}), f32[128,2,256]{2,1,0:T(2,128)S(1)}, u32[]{:S(2)}, u32[]{:S(2)}) async-start(f32[128,2,256]{2,1,0:T(2,128)} %broadcast_in_dim.2), calls=%async_computation.4 | async-start | bytes 524288 | tf_op jit(solution)/shard_map/all_to_all | solution.py:23
  134.4 4.5 %fusion.27 = bf16[512,4,256]{0,2,1:T(8,128)(2,1)} fusion(bf16[4,256,512]{1,2,0:T(8,128)(2,1)} %get-tuple-element.17, bf16[512,4,256]{2,1,0:T(4,128)(2,1)S(1)} %copy-done.3, bf16[512,512]{1,0:T(8,128)(2,1)S(1)} %copy-done, bf16[1,256,256]{2,1,0:T(8,128)(2,1)} %param.12), kind=kOutput, calls=%fused_computation.41 | convolution fusion | flops 816316416 | bytes 3801088 | tf_op jit(solution)/shard_map/ji,jhd->ihd/dot_general | solution.py:51
  141.8 4.3 %all-to-all-done.4 = f32[128,2,256]{2,1,0:T(2,128)S(1)} async-done(((f32[128,2,256]{2,1,0:T(2,128)}), f32[128,2,256]{2,1,0:T(2,128)S(1)}, u32[]{:S(2)}, u32[]{:S(2)}) %all-to-all-start.4) | async-done | bytes 262176 | tf_op jit(solution)/shard_map/all_to_all | solution.py:23
  146.1 9.2 %all-to-all-start.2 = ((bf16[128,4,1024]{2,1,0:T(4,128)(2,1)}), bf16[128,4,1024]{2,1,0:T(4,128)(2,1)S(1)}, u32[]{:S(2)}, u32[]{:S(2)}) async-start(bf16[128,4,1024]{2,1,0:T(4,128)(2,1)} %reshape.47), calls=%async_computation.2 | async-start | bytes 2097152 | tf_op jit(solution)/shard_map/all_to_all | solution.py:23
  155.3 2.3 %copy.56 = bf16[4,512,256]{1,2,0:T(8,128)(2,1)} copy(bf16[4,512,256]{2,1,0:T(8,128)(2,1)} %param.13) | data formatting | bytes 2097152 | tf_op args[6]
  158.5 26.4 %all-to-all-done.2 = bf16[128,4,1024]{2,1,0:T(4,128)(2,1)S(1)} async-done(((bf16[128,4,1024]{2,1,0:T(4,128)(2,1)}), bf16[128,4,1024]{2,1,0:T(4,128)(2,1)S(1)}, u32[]{:S(2)}, u32[]{:S(2)}) %all-to-all-start.2) | async-done | bytes 1048608 | tf_op jit(solution)/shard_map/all_to_all | solution.py:23
  186.9 4.1 %copy.67 = f32[4,4,128,256]{2,1,3,0:T(4,128)} copy(f32[4,4,128,256]{3,1,0,2:T(4,128)} %bitcast.107) | data formatting | bytes 4194304 | tf_op jit(solution)/shard_map/convert_element_type | solution.py:56
  191.0 3.1 %reshape.49 = f32[4,512,256]{1,2,0:T(8,128)} reshape(f32[4,4,128,256]{2,1,3,0:T(4,128)} %copy.67) | data formatting | bytes 4194304 | tf_op jit(solution)/shard_map/convert_element_type | solution.py:56
  194.1 3.8 %fusion.23 = (f32[4,512]{1,0:T(4,128)S(1)}, f32[4,256,512]{2,1,0:T(8,128)}) fusion(bf16[4,512,256]{1,2,0:T(8,128)(2,1)S(1)} %copy.57, f32[256]{0:T(256)S(1)} %copy-done.6, bf16[512,512]{1,0:T(8,128)(2,1)S(1)} %copy-done.4, f32[4,512,256]{1,2,0:T(8,128)} %reshape.49, f32[4,512]{1,0:T(4,128)S(1)} %copy-done.5), kind=kOutput, calls=%fused_computation.32 | convolution fusion | flops 540014592 | bytes 5784576 | tf_op jit(solution)/shard_map/ji,rjd->rid/dot_general | solution.py:57
  197.8 11.2 %psum.15 = f32[4,512]{1,0:T(4,128)S(1)} all-reduce(f32[4,512]{1,0:T(4,128)S(1)} %get-tuple-element.14), channel_id=1, replica_groups=mesh['seq'=128,'chan'=4] {'chan'}, use_global_device_ids=true, to_apply=%region_3.0 | all-reduce | flops 2048 | bytes 16384 | tf_op jit(solution)/shard_map/psum | solution.py:58
  209.0 3.3 %fusion.22 = bf16[4,512,256]{1,2,0:T(8,128)(2,1)} fusion(bf16[4,512,256]{1,2,0:T(8,128)(2,1)S(1)} %copy.57, f32[4,256,512]{2,1,0:T(8,128)} %get-tuple-element.15, bf16[4,512,256]{1,2,0:T(8,128)(2,1)S(1)} %copy-done.2, f32[4,512]{1,0:T(4,128)S(1)} %psum.15, f32[4,512]{1,0:T(4,128)S(1)} %get-tuple-element.12, f32[256]{0:T(256)S(1)} %copy-done.6, ...), kind=kLoop, calls=%fused_computation.31 | loop fusion | flops 5242880 | bytes 5268480 | tf_op jit(solution)/shard_map/convert_element_type | solution.py:67
  212.3 2.3 %copy.72 = bf16[4,512,256]{2,1,0:T(8,128)(2,1)} copy(bf16[4,512,256]{1,2,0:T(8,128)(2,1)} %fusion.22) | data formatting | bytes 2097152
  (28 shorter events, 13.1 us)
Async XLA Ops:
  0.6 74.2 %copy-start = (bf16[512,512]{1,0:T(8,128)(2,1)S(1)}, bf16[512,512]{1,0:T(8,128)(2,1)}, u32[]{:S(2)}) copy-start(bf16[512,512]{1,0:T(8,128)(2,1)} %param.10) | copy-start | bytes 1572868
  0.6 17.7 %copy-start.6 = (f32[256]{0:T(256)S(1)}, f32[256]{0:T(256)}, u32[]{:S(2)}) copy-start(f32[256]{0:T(256)} %param.8) | copy-start | bytes 3076
  0.7 17.7 %copy-start.5 = (f32[4,512]{1,0:T(4,128)S(1)}, f32[4,512]{1,0:T(4,128)}, u32[]{:S(2)}) copy-start(f32[4,512]{1,0:T(4,128)} %param.11) | copy-start | bytes 24580
  0.7 17.7 %copy-start.4 = (bf16[512,512]{1,0:T(8,128)(2,1)S(1)}, bf16[512,512]{1,0:T(8,128)(2,1)}, u32[]{:S(2)}) copy-start(bf16[512,512]{1,0:T(8,128)(2,1)} %param.9) | copy-start | bytes 1572868
  20.4 15.8 %copy-start.1 = (bf16[4,512,256]{2,1,0:T(8,128)(2,1)S(1)}, bf16[4,512,256]{2,1,0:T(8,128)(2,1)}, u32[]{:S(2)}) copy-start(bf16[4,512,256]{2,1,0:T(8,128)(2,1)} %param.13) | copy-start | bytes 3145732
  23.2 41.5 %all-to-all-start.1 = ((bf16[128,4,1024]{2,1,0:T(4,128)(2,1)}), bf16[128,4,1024]{2,1,0:T(4,128)(2,1)}, u32[]{:S(2)}, u32[]{:S(2)}) async-start(bf16[128,4,1024]{2,1,0:T(4,128)(2,1)} %copy.62), calls=%async_computation.1 | async-start | bytes 2097152 | tf_op jit(solution)/shard_map/all_to_all | solution.py:23
  64.7 37.7 %all-to-all-start = ((bf16[128,4,1024]{2,1,0:T(4,128)(2,1)}), bf16[128,4,1024]{2,1,0:T(4,128)(2,1)S(1)}, u32[]{:S(2)}, u32[]{:S(2)}) async-start(bf16[128,4,1024]{2,1,0:T(4,128)(2,1)} %copy.59), calls=%async_computation | async-start | bytes 2097152 | tf_op jit(solution)/shard_map/all_to_all | solution.py:23
  103.5 30.8 %copy-start.3 = (bf16[512,4,256]{2,1,0:T(4,128)(2,1)S(1)}, bf16[512,4,256]{2,1,0:T(4,128)(2,1)}, u32[]{:S(2)}) copy-start(bf16[512,4,256]{2,1,0:T(4,128)(2,1)} %reshape.43) | copy-start | bytes 3145732
  125.7 20.4 %all-to-all-start.4 = ((f32[128,2,256]{2,1,0:T(2,128)}), f32[128,2,256]{2,1,0:T(2,128)S(1)}, u32[]{:S(2)}, u32[]{:S(2)}) async-start(f32[128,2,256]{2,1,0:T(2,128)} %broadcast_in_dim.2), calls=%async_computation.4 | async-start | bytes 524288 | tf_op jit(solution)/shard_map/all_to_all | solution.py:23
  146.1 38.8 %all-to-all-start.2 = ((bf16[128,4,1024]{2,1,0:T(4,128)(2,1)}), bf16[128,4,1024]{2,1,0:T(4,128)(2,1)S(1)}, u32[]{:S(2)}, u32[]{:S(2)}) async-start(bf16[128,4,1024]{2,1,0:T(4,128)(2,1)} %reshape.47), calls=%async_computation.2 | async-start | bytes 2097152 | tf_op jit(solution)/shard_map/all_to_all | solution.py:23
  194.1 15.0 %copy-start.2 = (bf16[4,512,256]{1,2,0:T(8,128)(2,1)S(1)}, bf16[4,512,256]{1,2,0:T(8,128)(2,1)}, u32[]{:S(2)}) copy-start(bf16[4,512,256]{1,2,0:T(8,128)(2,1)} %copy.56) | copy-start | bytes 3145732

commit v2 on v1

v2 whole, which is shorter than its diff:
```python
import functools

import jax
import jax.numpy as jnp
from jax import lax
from jax.experimental import pallas as pl
from jax.experimental.pallas import tpu as pltpu
from jax.sharding import PartitionSpec as P

D = 1024
GELU_C = 0.7978845608028654
GELU_A = 0.044715
F32 = jnp.float32
BF16 = jnp.bfloat16
LANES = 128


def dot(a, b, ca, cb):
    return lax.dot_general(a, b, (((ca,), (cb,)), ((), ())), preferred_element_type=F32)


def lane_sums(v):
    ones = jnp.ones((8, v.shape[1]), BF16)
    hi = v.astype(BF16)
    rest = v - hi.astype(F32)
    return dot(ones, hi, 1, 1) + dot(ones, rest.astype(BF16), 1, 1)


def column_form(v):
    r, n = v.shape
    return jnp.concatenate([v] * (8 // r), axis=0).T


class Sizes:
    def __init__(self, seq, rows, n2, width):
        self.seq, self.rows, self.n2, self.width = seq, rows, n2, width
        self.cols = n2 // seq
        self.parts = width // LANES
        self.block = self.cols * self.parts * rows
        self.extra = 2 * (width // seq) * self.parts

    def pieces(self):
        for jh in range(self.cols):
            for part in range(self.parts):
                yield jh, part, (jh * self.parts + part) * self.rows


def square_kernel(s, x_ref, sum_ref):
    for r in range(s.rows):
        x = x_ref[r].astype(F32)
        sum_ref[r : r + 1, :] = lane_sums(x * x)[0:1]


def inner_kernel(s, x_ref, cot_ref, sum_ref, gain_ref, inner_ref, tw_ref, send_ref, inv_ref, wide_ref):
    inv = lax.rsqrt(sum_ref[...] / D + 1e-05)
    inv_ref[...] = inv
    inv_cols = column_form(inv)
    tw_cols = column_form(tw_ref[...])
    for r in range(s.rows):
        normed = (x_ref[r].astype(F32) * inv_cols[:, r : r + 1] * gain_ref[...]).astype(BF16)
        y = dot(inner_ref[...], normed, 1, 0) * tw_cols[:, r : r + 1]
        cot = cot_ref[r].astype(F32)
        for jh, part, q in s.pieces():
            here = slice(jh * s.seq, (jh + 1) * s.seq), slice(part * LANES, (part + 1) * LANES)
            wide_ref[pl.ds(q + r, s.seq, 2 * s.block), :] = y[here]
            wide_ref[pl.ds(s.block + q + r, s.seq, 2 * s.block), :] = cot[here]
    send_ref[...] = wide_ref[...].astype(BF16)


def swap_halves(first, second):
    low = lax.broadcasted_iota(jnp.int32, first.shape, 1) < 4
    return (
        jnp.where(low, first, pltpu.roll(second, 4, 1)),
        jnp.where(low, pltpu.roll(first, 4, 1), second),
    )


def unit(n):
    a = lax.broadcasted_iota(jnp.int32, (n, n), 0)
    return jnp.where(a == lax.broadcasted_iota(jnp.int32, (n, n), 1), 1.0, 0.0).astype(BF16)


def middle_kernel(s, got_ref, weight_ref, outer_ref, send_ref, part_ref, out_ref):
    n1 = s.seq * s.rows
    outer_t = dot(unit(n1), outer_ref[...], 1, 1).astype(BF16)
    tiles = s.block // 8
    got = got_ref[...].reshape(s.seq // 2, 2, 2 * tiles, 8, LANES)
    for jh in range(s.cols):
        rot, cot = (
            jnp.concatenate(
                [
                    v.reshape(n1, LANES)
                    for v in swap_halves(got[:, 0, tile].astype(F32), got[:, 1, tile].astype(F32))
                ],
                axis=1,
            ).astype(BF16)
            for tile in (jh, tiles + jh)
        )
        v = dot(outer_ref[...], rot, 1, 0).astype(BF16).astype(F32)
        t = jnp.tanh(GELU_C * (v + GELU_A * v * v * v))
        hidden = (0.5 * v * (1.0 + t)).astype(BF16)
        slope = 0.5 * (1.0 + t) + 0.5 * v * (1.0 - t * t) * GELU_C * (1.0 + 3.0 * GELU_A * v * v)
        grad = (dot(cot, weight_ref[...], 1, 1) * slope).astype(BF16)
        product = dot(hidden, cot, 0, 0)
        for part in range(s.parts):
            here = slice(part * s.width, (part + 1) * s.width)
            term = product[:, part * LANES : (part + 1) * LANES]
            part_ref[here, :] = term if jh == 0 else part_ref[here, :] + term
        back = dot(outer_t, grad, 1, 0)
        even, odd = swap_halves(
            back[:, :LANES].reshape(n1 // 8, 8, LANES), back[:, LANES:].reshape(n1 // 8, 8, LANES)
        )
        out_ref[:, 0, jh] = even
        out_ref[:, 1, jh] = odd
    step = s.width // s.seq
    flat = out_ref.reshape(s.seq * (s.block + s.extra), LANES)
    for i in range(step):
        for part in range(s.parts):
            at = s.block + i * s.parts + part
            v = part_ref[pl.ds(part * s.width + i, s.seq, step), :]
            hi = v.astype(BF16).astype(F32)
            flat[pl.ds(at, s.seq, s.block + s.extra), :] = hi
            flat[pl.ds(at + s.extra // 2, s.seq, s.block + s.extra), :] = v - hi
    send_ref[...] = flat[...].astype(BF16)


def back_kernel(s, got_ref, x_ref, cot_ref, inv_ref, gain_ref, tw_ref, inner_ref, sum_ref, proj_ref, wide_ref, col_ref):
    inner_t = dot(unit(s.n2), inner_ref[...], 1, 1).astype(BF16)
    wide_ref[...] = got_ref[...].astype(F32)
    full = s.block + s.extra
    inv_cols = column_form(inv_ref[...])
    tw_cols = column_form(tw_ref[...])
    for r in range(s.rows):
        for jh, part, q in s.pieces():
            here = slice(jh * s.seq, (jh + 1) * s.seq)
            col_ref[here, part * LANES : (part + 1) * LANES] = (
                wide_ref[pl.ds(q + r, s.seq, full), :] * tw_cols[here, r : r + 1]
            ).astype(BF16)
        grad = dot(inner_t, col_ref[...], 1, 0)
        gained = grad * gain_ref[...]
        proj_ref[r : r + 1, :] = lane_sums(gained * x_ref[r].astype(F32))[0:1]
        sum_ref[r] = cot_ref[r].astype(F32) + inv_cols[:, r : r + 1] * gained


def finish_kernel(s, sum_ref, x_ref, inv_ref, proj_ref, whole_ref, out_ref, weight_ref):
    for part in range(s.parts):
        weight_ref[:, part * LANES : (part + 1) * LANES] = whole_ref[pl.ds(part, s.width, s.parts), :]
    inv = inv_ref[...]
    factor = column_form(inv * inv * inv * proj_ref[...] / D)
    for r in range(s.rows):
        out_ref[r] = (sum_ref[r] - x_ref[r].astype(F32) * factor[:, r : r + 1]).astype(BF16)


def call(kernel, s, name, outs, scratch, flops, moved, *args):
    return pl.pallas_call(
        functools.partial(kernel, s),
        out_shape=[jax.ShapeDtypeStruct(shape, kind) for shape, kind in outs],
        scratch_shapes=[pltpu.VMEM(shape, kind) for shape, kind in scratch],
        compiler_params=pltpu.CompilerParams(vmem_limit_bytes=60 << 20),
        cost_estimate=pl.CostEstimate(flops=flops, bytes_accessed=moved, transcendentals=0),
        name=name,
    )(*args)


def exchange(v, seq):
    packed = v.reshape(seq, -1, LANES)
    return lax.all_to_all(packed, "seq", split_axis=0, concat_axis=0, tiled=True).reshape(v.shape)


def on_device(seq, inputs, norm_gain, inner_factor, outer_factor, twiddle, channel_weight, cotangent):
    rows, n2, width = inputs.shape
    s = Sizes(seq, rows, n2, width)
    packed_two = (2 * seq * s.block, LANES)
    packed_more = (seq * (s.block + s.extra), LANES)
    mib = rows * n2 * width * 2
    flop = 2 * rows * n2 * n2 * width
    gain = norm_gain.reshape(1, width)
    weight = channel_weight[0]
    (part_sum,) = call(square_kernel, s, "squares", [((rows, n2), F32)], [], flop // 20, mib, inputs)
    sq_sum = lax.psum(part_sum, "chan")
    send, inv = call(
        inner_kernel, s, "inner", [(packed_two, BF16), ((rows, n2), F32)], [(packed_two, F32)], flop, 5 * mib,
        inputs, cotangent, sq_sum, gain, inner_factor, twiddle,
    )
    got = exchange(send, seq)
    (back_send,) = call(
        middle_kernel, s, "middle", [(packed_more, BF16)],
        [((s.parts * width, LANES), F32), ((seq // 2, 2, (s.block + s.extra) // 8, 8, LANES), F32)], 3 * flop, 4 * mib,
        got, weight, outer_factor,
    )
    back_got = exchange(back_send, seq)
    pairs = back_got.reshape(seq, s.block + s.extra, LANES)[:, s.block :].astype(F32)
    pairs = jnp.sum(pairs, axis=0)
    share = pairs[: s.extra // 2] + pairs[s.extra // 2 :]
    whole = lax.all_to_all(
        jnp.broadcast_to(share, (seq,) + share.shape), "seq", split_axis=0, concat_axis=0, tiled=True
    )
    base, part_proj = call(
        back_kernel, s, "back", [(inputs.shape, F32), ((rows, n2), F32)],
        [(packed_more, F32), ((n2, width), BF16)], flop, 6 * mib,
        back_got, inputs, cotangent, inv, gain, twiddle, inner_factor,
    )
    projection = lax.psum(part_proj, "chan")
    input_grad, weight_grad = call(
        finish_kernel, s, "finish", [(inputs.shape, BF16), ((width, width), F32)], [], flop // 100, 4 * mib,
        base, inputs, inv, projection, whole.reshape(-1, LANES),
    )
    return (input_grad, weight_grad.reshape(1, width, width))


def solution(mesh):
    in_specs = (
        P("seq", None, "chan"),
        P("chan"),
        P(),
        P(),
        P("seq", None),
        P("chan", None, None),
        P("seq", None, "chan"),
    )
    out_specs = (P("seq", None, "chan"), P("chan", None, None))

    def run(*args):
        return on_device(mesh.shape["seq"], *args)

    return jax.shard_map(run, mesh=mesh, in_specs=in_specs, out_specs=out_specs, check_vma=False)
```

time: 215 us -> 171 us (0.80)
  blocking collectives: 45.7 us -> 135 us
  waiting for transfers between devices: 76.5 us -> 0.01 us
  local copies, waits for them, and re-layouts: 34.1 us -> 1.64 us
  starting transfers between devices: 38.7 us -> 6.89 us
  Pallas kernels: 0 us -> 25.5 us
  matrix products: 15.1 us -> 0 us
  other arithmetic: 3.68 us -> 0.14 us
    all_to_all x1 -> x2, blocking collectives: 18.6 us -> 107 us  [exchange(): lax.all_to_all(packed, 'seq', split_axis=0, concat_axis=0, tiled=True)]
    all_to_all x4 -> x1, waiting for transfers between devices: 76.5 us -> 0.01 us  [on_device(): lax.all_to_all(jnp.broadcast_to(share, (seq,) + share.shape), 'seq', spli...]
    all_to_all x4 -> x1, starting transfers between devices: 38.7 us -> 6.89 us  [on_device(): lax.all_to_all(jnp.broadcast_to(share, (seq,) + share.shape), 'seq', spli...]
    pallas_call x0 -> x5, Pallas kernels: none -> 25.5 us  [call(): pl.pallas_call(functools.partial(kernel, s), out_shape=[jax.ShapeDtypeStr...]
    dot_general x5 -> x0, matrix products: 15.1 us -> none  [the longest x1 4.55 us: on_device(): jnp.einsum('ji,jhd->ihd', outer_factor, mixed_grad, preferred_element_typ...]
    convert_element_type x5 -> x0, local copies, waits for them, and re-layouts: 13.4 us -> none  [the longest x3 9.08 us: on_device(): back.astype(jnp.float32)]
    reshape x7 -> x0, local copies, waits for them, and re-layouts: 12.2 us -> none  [the longest x4 8.91 us: to_columns(): return exchange(v.reshape(seq, r, -1)).reshape(seq * r, n2 // seq, d)]
    unnamed x17 -> x4, local copies, waits for them, and re-layouts: 6.17 us -> 0.73 us
  transfers between devices with their start and end apart: 4 -> 1, of which waited for: 4 -> 0; matrix products, arithmetic and copies ran while one was open for 11% -> 0% of each run, Pallas kernels for 0% -> 4%
where the time goes in v2:
time: 171 us; the launch traced here: 170 us
  blocking collectives  135 us (79%)
  Pallas kernels  25.5 us (15%)
  starting transfers between devices  6.89 us (4%)
    all_to_all x2, blocking collectives, exchange(): lax.all_to_all(packed, 'seq', split_axis=0, concat_axis=0, tiled=True)  107 us
    pallas_call x5, Pallas kernels, call(): pl.pallas_call(functools.partial(kernel, s), out_shape=[jax.ShapeDtypeStr...  25.5 us
    psum x1, blocking collectives, on_device(): sq_sum = lax.psum(part_sum, 'chan')  16.6 us
    psum x1, blocking collectives, on_device(): projection = lax.psum(part_proj, 'chan')  11.1 us
    all_to_all x1, starting transfers between devices, on_device(): lax.all_to_all(jnp.broadcast_to(share, (seq,) + share.shape), 'seq', spli...  6.89 us
  transfers between devices with their start and end apart: 1, of which 0 were waited for; matrix products, arithmetic and copies ran while one was open for 0% of the time, Pallas kernels for 4%

profile of v2, /device:TPU:1, one launch (start us, length us, event | category | flops | bytes accessed | tf_op | source)
XLA Modules:
  0.0 169.6 jit_solution(16193774592270459431)
XLA Ops:
  0.6 2.5 %squares.1 = f32[4,512]{1,0:T(4,128)} custom-call(bf16[4,512,256]{2,1,0:T(8,128)(2,1)} %x_ref.7), custom_call_target="tpu_custom_call" | custom-call | flops 26843544 | bytes 1048576 | tf_op jit(solution)/shard_map/squares/pallas_call | solution.py:155
  3.1 16.6 %psum.14.sum_ref = f32[4,512]{1,0:T(4,128)} all-reduce(f32[4,512]{1,0:T(4,128)} %squares.1), channel_id=1, replica_groups=mesh['seq'=128,'chan'=4] {'chan'}, use_global_device_ids=true, to_apply=%region_0.0 | all-reduce | flops 2048 | bytes 16384 | tf_op jit(solution)/shard_map/psum | solution.py:180
  19.7 7.0 %inner.1 = (bf16[8192,128]{1,0:T(8,128)(2,1)}, f32[4,512]{1,0:T(4,128)}) custom-call(bf16[4,512,256]{2,1,0:T(8,128)(2,1)} %x_ref.7, bf16[4,512,256]{2,1,0:T(8,128)(2,1)} %cot_ref.3, f32[4,512]{1,0:T(4,128)} %psum.14.sum_ref, f32[1,256]{1,0:T(1,128)} %bitcast.13, bf16[512,512]{1,0:T(8,128)(2,1)} %inner_ref.3, f32[4,512]{1,0:T(4,128)} %tw_ref.3), custom_call_target="tpu_custom_call" | custom-call | flops 536870912 | bytes 5242880 | tf_op jit(solution)/shard_map/inner/pallas_call | solution.py:155
  26.7 63.8 %all_to_all.15 = bf16[128,64,128]{2,1,0:T(8,128)(2,1)} all-to-all(bf16[128,64,128]{2,1,0:T(8,128)(2,1)} %bitcast.9), channel_id=1, replica_groups=mesh['seq'=128,'chan'=4] {'seq'}, dimensions={0} | all-to-all | bytes 4194304 | tf_op jit(solution)/shard_map/all_to_all | solution.py:167
  90.5 6.3 %middle.1 = bf16[5120,128]{1,0:T(8,128)(2,1)} custom-call(bf16[8192,128]{1,0:T(8,128)(2,1)} %bitcast.10, bf16[256,256]{1,0:T(8,128)(2,1)} %bitcast.16, bf16[512,512]{1,0:T(8,128)(2,1)} %outer_ref.1), custom_call_target="tpu_custom_call" | custom-call | flops 1610612736 | bytes 4194304 | tf_op jit(solution)/shard_map/middle/pallas_call | solution.py:155
  96.9 43.2 %all_to_all.16 = bf16[128,40,128]{2,1,0:T(8,128)(2,1)S(1)} all-to-all(bf16[128,40,128]{2,1,0:T(8,128)(2,1)} %bitcast.11), channel_id=1, replica_groups=mesh['seq'=128,'chan'=4] {'seq'}, dimensions={0} | all-to-all | bytes 2621440 | tf_op jit(solution)/shard_map/all_to_all | solution.py:167
  140.1 0.0 copy-start
  140.1 0.1 convert_reduce_fusion
  140.2 0.9 broadcast_in_dim.3
  141.2 6.9 %all-to-all-start.2 = ((f32[128,4,128]{2,1,0:T(4,128)}), f32[128,4,128]{2,1,0:T(4,128)S(1)}, u32[]{:S(2)}, u32[]{:S(2)}) async-start(f32[128,4,128]{2,1,0:T(4,128)} %broadcast_in_dim.3), calls=%async_computation.2 | async-start | bytes 524288 | tf_op jit(solution)/shard_map/all_to_all | solution.py:195
  148.1 0.0 copy-done
  148.1 6.2 %back.1 = (f32[4,512,256]{2,1,0:T(8,128)}, f32[4,512]{1,0:T(4,128)}) custom-call(bf16[5120,128]{1,0:T(8,128)(2,1)} %bitcast.8, bf16[4,512,256]{2,1,0:T(8,128)(2,1)} %x_ref.7, bf16[4,512,256]{2,1,0:T(8,128)(2,1)} %cot_ref.3, f32[4,512]{1,0:T(4,128)} %get-tuple-element.9.inv_ref, f32[1,256]{1,0:T(1,128)} %bitcast.14, f32[4,512]{1,0:T(4,128)} %tw_ref.3, ...), custom_call_target="tpu_custom_call" | custom-call | flops 536870912 | bytes 6291456 | tf_op jit(solution)/shard_map/back/pallas_call | solution.py:155
  154.3 11.1 %psum.15.proj_ref = f32[4,512]{1,0:T(4,128)} all-reduce(f32[4,512]{1,0:T(4,128)} %get-tuple-element.11), channel_id=1, replica_groups=mesh['seq'=128,'chan'=4] {'chan'}, use_global_device_ids=true, to_apply=%region_1.0 | all-reduce | flops 2048 | bytes 16384 | tf_op jit(solution)/shard_map/psum | solution.py:203
  165.4 0.0 all-to-all-done.2
  165.4 0.0 copy-start.1
  165.4 0.7 copy-done.1
  166.2 3.4 %finish.1 = (bf16[4,512,256]{2,1,0:T(8,128)(2,1)}, f32[256,256]{1,0:T(8,128)}) custom-call(f32[4,512,256]{2,1,0:T(8,128)} %get-tuple-element.10.sum_ref, bf16[4,512,256]{2,1,0:T(8,128)(2,1)} %x_ref.7, f32[4,512]{1,0:T(4,128)} %get-tuple-element.9.inv_ref, f32[4,512]{1,0:T(4,128)} %psum.15.proj_ref, f32[512,128]{1,0:T(8,128)} %bitcast.12), custom_call_target="tpu_custom_call" | custom-call | flops 5368709 | bytes 4194304 | tf_op jit(solution)/shard_map/finish/pallas_call | solution.py:155
  (1 shorter events, 0.0 us)
Async XLA Ops:
  140.1 8.0 %copy-start = (bf16[128,40,128]{2,1,0:T(8,128)(2,1)}, bf16[128,40,128]{2,1,0:T(8,128)(2,1)S(1)}, u32[]{:S(2)}) copy-start(bf16[128,40,128]{2,1,0:T(8,128)(2,1)S(1)} %all_to_all.16) | copy-start | bytes 3932164
  141.2 24.3 %all-to-all-start.2 = ((f32[128,4,128]{2,1,0:T(4,128)}), f32[128,4,128]{2,1,0:T(4,128)S(1)}, u32[]{:S(2)}, u32[]{:S(2)}) async-start(f32[128,4,128]{2,1,0:T(4,128)} %broadcast_in_dim.3), calls=%async_computation.2 | async-start | bytes 524288 | tf_op jit(solution)/shard_map/all_to_all | solution.py:195
  165.4 0.7 copy-start.1

commit v3 on v2

v3 whole, which is shorter than its diff:
```python
import functools

import jax
import jax.numpy as jnp
from jax import lax
from jax.experimental import pallas as pl
from jax.experimental.pallas import tpu as pltpu
from jax.sharding import PartitionSpec as P

D = 1024
GELU_C = 0.7978845608028654
GELU_A = 0.044715
F32 = jnp.float32
BF16 = jnp.bfloat16
LANES = 128
CHUNKS = 4


def dot(a, b, ca, cb):
    return lax.dot_general(a, b, (((ca,), (cb,)), ((), ())), preferred_element_type=F32)


def lane_sums(v):
    ones = jnp.ones((8, v.shape[1]), BF16)
    hi = v.astype(BF16)
    rest = v - hi.astype(F32)
    return dot(ones, hi, 1, 1) + dot(ones, rest.astype(BF16), 1, 1)


def column_form(v):
    r, n = v.shape
    return jnp.concatenate([v] * (8 // r), axis=0).T


class Sizes:
    def __init__(self, seq, rows, n2, width):
        self.seq, self.rows, self.n2, self.width = seq, rows, n2, width
        self.cols = n2 // seq
        self.parts = width // LANES
        self.block = self.cols * self.parts * rows
        self.extra = 2 * (width // seq) * self.parts

    def pieces(self):
        for jh in range(self.cols):
            for part in range(self.parts):
                yield jh, part, (jh * self.parts + part) * self.rows


class Copies:
    def __init__(self, sems):
        self.sems, self.all = sems, []

    def start(self, source, target):
        copy = pltpu.make_async_copy(source, target, self.sems.at[len(self.all)])
        copy.start()
        self.all.append(copy)
        return copy

    def rows(self, source, target, count):
        return [self.start(source.at[r], target.at[r]) for r in range(count)]


def wait(copies):
    for copy in copies:
        copy.wait()


def square_kernel(s, x_hbm, sum_ref, x_ref, sems):
    loads = Copies(sems).rows(x_hbm, x_ref, s.rows)
    for r in range(s.rows):
        loads[r].wait()
        x = x_ref[r].astype(F32)
        sum_ref[r : r + 1, :] = lane_sums(x * x)[0:1]


def inner_kernel(
    s, x_hbm, cot_hbm, inner_hbm, sum_ref, gain_ref, tw_ref, send_hbm, inv_ref,
    x_ref, cot_ref, inner_ref, wide_ref, wide_cot_ref, buf_ref, buf_cot_ref, sems,
):
    copies = Copies(sems)
    cot_loads = copies.rows(cot_hbm, cot_ref, s.rows)
    inner_load = copies.start(inner_hbm, inner_ref)
    x_loads = copies.rows(x_hbm, x_ref, s.rows)
    inv = lax.rsqrt(sum_ref[...] / D + 1e-05)
    inv_ref[...] = inv
    inv_cols = column_form(inv)
    tw_cols = column_form(tw_ref[...])
    for r in range(s.rows):
        cot_loads[r].wait()
        for jh, part, q in s.pieces():
            wide_cot_ref[pl.ds(q + r, s.seq, s.block), :] = cot_ref[
                r, jh * s.seq : (jh + 1) * s.seq, part * LANES : (part + 1) * LANES
            ].astype(F32)
    buf_cot_ref[...] = wide_cot_ref[...].astype(BF16).reshape(buf_cot_ref.shape)
    stores = [copies.start(buf_cot_ref, send_hbm.at[:, s.block : 2 * s.block])]
    inner_load.wait()
    for r in range(s.rows):
        x_loads[r].wait()
        normed = (x_ref[r].astype(F32) * inv_cols[:, r : r + 1] * gain_ref[...]).astype(BF16)
        y = dot(inner_ref[...], normed, 1, 0) * tw_cols[:, r : r + 1]
        for jh, part, q in s.pieces():
            wide_ref[pl.ds(q + r, s.seq, s.block), :] = y[
                jh * s.seq : (jh + 1) * s.seq, part * LANES : (part + 1) * LANES
            ]
    some = s.seq // CHUNKS
    for k in range(CHUNKS):
        here = slice(k * some, (k + 1) * some)
        wide = wide_ref[k * some * s.block : (k + 1) * some * s.block, :].astype(BF16)
        buf_ref[here] = wide.reshape(some, s.block, LANES)
        stores.append(copies.start(buf_ref.at[here], send_hbm.at[here, 0 : s.block]))
    wait(stores)


def swap_halves(first, second):
    low = lax.broadcasted_iota(jnp.int32, first.shape, 1) < 4
    return (
        jnp.where(low, first, pltpu.roll(second, 4, 1)),
        jnp.where(low, pltpu.roll(first, 4, 1), second),
    )


def unit(n):
    a = lax.broadcasted_iota(jnp.int32, (n, n), 0)
    return jnp.where(a == lax.broadcasted_iota(jnp.int32, (n, n), 1), 1.0, 0.0).astype(BF16)


def sources(s, got_ref, k, tile):
    got = got_ref[k].astype(F32).reshape(s.seq // 2, 2, s.block // 16, 8, LANES)
    return got[:, 0, tile], got[:, 1, tile]


def middle_kernel(
    s, got_hbm, outer_hbm, weight_ref, send_hbm, got_ref, outer_ref, part_ref, out_ref, buf_ref, sems
):
    n1 = s.seq * s.rows
    copies = Copies(sems)
    outer_load = copies.start(outer_hbm, outer_ref)
    loads = {}
    half = s.block // 2
    for k in (0, 2, 1, 3):
        loads[k] = copies.start(got_hbm.at[:, k * half : (k + 1) * half], got_ref.at[k])
    outer_load.wait()
    outer_t = dot(unit(n1), outer_ref[...], 1, 1).astype(BF16)
    for jh in range(s.cols):
        if jh % 2 == 0:
            loads[jh // 2].wait()
            loads[2 + jh // 2].wait()
        rot, cot = (
            jnp.concatenate(
                [v.reshape(n1, LANES) for v in swap_halves(*sources(s, got_ref, k, jh % 2))], axis=1
            ).astype(BF16)
            for k in (jh // 2, 2 + jh // 2)
        )
        v = dot(outer_ref[...], rot, 1, 0).astype(BF16).astype(F32)
        t = jnp.tanh(GELU_C * (v + GELU_A * v * v * v))
        hidden = (0.5 * v * (1.0 + t)).astype(BF16)
        slope = 0.5 * (1.0 + t) + 0.5 * v * (1.0 - t * t) * GELU_C * (1.0 + 3.0 * GELU_A * v * v)
        grad = (dot(cot, weight_ref[...], 1, 1) * slope).astype(BF16)
        product = dot(hidden, cot, 0, 0)
        for part in range(s.parts):
            here = slice(part * s.width, (part + 1) * s.width)
            term = product[:, part * LANES : (part + 1) * LANES]
            part_ref[here, :] = term if jh == 0 else part_ref[here, :] + term
        back = dot(outer_t, grad, 1, 0)
        even, odd = swap_halves(
            back[:, :LANES].reshape(n1 // 8, 8, LANES), back[:, LANES:].reshape(n1 // 8, 8, LANES)
        )
        out_ref[:, 0, jh] = even
        out_ref[:, 1, jh] = odd
    step = s.width // s.seq
    flat = out_ref.reshape(s.seq * (s.block + s.extra), LANES)
    for i in range(step):
        for part in range(s.parts):
            at = s.block + i * s.parts + part
            v = part_ref[pl.ds(part * s.width + i, s.seq, step), :]
            hi = v.astype(BF16).astype(F32)
            flat[pl.ds(at, s.seq, s.block + s.extra), :] = hi
            flat[pl.ds(at + s.extra // 2, s.seq, s.block + s.extra), :] = v - hi
    some = s.seq // CHUNKS
    full = s.block + s.extra
    stores = []
    for k in range(CHUNKS):
        here = slice(k * some, (k + 1) * some)
        buf_ref[here] = flat[k * some * full : (k + 1) * some * full, :].astype(BF16).reshape(some, full, LANES)
        stores.append(copies.start(buf_ref.at[here], send_hbm.at[here]))
    wait(stores)


def back_kernel(
    s, got_hbm, x_hbm, cot_hbm, inner_hbm, inv_ref, gain_ref, tw_ref, sum_hbm, proj_ref,
    got_ref, x_ref, cot_ref, inner_ref, sum_ref, wide_ref, col_ref, sems,
):
    copies = Copies(sems)
    some = s.seq // CHUNKS
    slices = [slice(k * some, (k + 1) * some) for k in range(CHUNKS)]
    got_loads = [copies.start(got_hbm.at[here], got_ref.at[here]) for here in slices]
    inner_load = copies.start(inner_hbm, inner_ref)
    x_loads = copies.rows(x_hbm, x_ref, s.rows)
    cot_loads = copies.rows(cot_hbm, cot_ref, s.rows)
    full = s.block + s.extra
    inv_cols = column_form(inv_ref[...])
    tw_cols = column_form(tw_ref[...])
    for k in range(CHUNKS):
        got_loads[k].wait()
        wide_ref[k * some * full : (k + 1) * some * full, :] = (
            got_ref[slices[k]].astype(F32).reshape(some * full, LANES)
        )
    inner_load.wait()
    inner_t = dot(unit(s.n2), inner_ref[...], 1, 1).astype(BF16)
    stores = []
    for r in range(s.rows):
        for jh, part, q in s.pieces():
            here = slice(jh * s.seq, (jh + 1) * s.seq)
            col_ref[here, part * LANES : (part + 1) * LANES] = (
                wide_ref[pl.ds(q + r, s.seq, full), :] * tw_cols[here, r : r + 1]
            ).astype(BF16)
        grad = dot(inner_t, col_ref[...], 1, 0)
        gained = grad * gain_ref[...]
        x_loads[r].wait()
        proj_ref[r : r + 1, :] = lane_sums(gained * x_ref[r].astype(F32))[0:1]
        cot_loads[r].wait()
        sum_ref[r] = cot_ref[r].astype(F32) + inv_cols[:, r : r + 1] * gained
        stores.append(copies.start(sum_ref.at[r], sum_hbm.at[r]))
    wait(stores)


def finish_kernel(s, sum_hbm, x_hbm, inv_ref, proj_ref, whole_ref, out_hbm, weight_ref, sum_ref, x_ref, out_ref, sems):
    copies = Copies(sems)
    loads = []
    for r in range(s.rows):
        loads.append([copies.start(sum_hbm.at[r], sum_ref.at[r]), copies.start(x_hbm.at[r], x_ref.at[r])])
    inv = inv_ref[...]
    factor = column_form(inv * inv * inv * proj_ref[...] / D)
    stores = []
    for r in range(s.rows):
        wait(loads[r])
        out_ref[r] = (sum_ref[r] - x_ref[r].astype(F32) * factor[:, r : r + 1]).astype(BF16)
        stores.append(copies.start(out_ref.at[r], out_hbm.at[r]))
    for part in range(s.parts):
        weight_ref[:, part * LANES : (part + 1) * LANES] = whole_ref[pl.ds(part, s.width, s.parts), :]
    wait(stores)


def call(kernel, s, name, outs, scratch, copies, flops, moved, far, near):
    hbm, vmem = pl.BlockSpec(memory_space=pl.ANY), pl.BlockSpec(memory_space=pltpu.VMEM)
    return pl.pallas_call(
        functools.partial(kernel, s),
        out_shape=[jax.ShapeDtypeStruct(shape, kind) for shape, kind in outs],
        in_specs=[hbm] * len(far) + [vmem] * len(near),
        out_specs=[hbm if len(shape) == 3 else vmem for shape, _ in outs],
        scratch_shapes=[pltpu.VMEM(shape, kind) for shape, kind in scratch]
        + [pltpu.SemaphoreType.DMA((copies,))],
        compiler_params=pltpu.CompilerParams(vmem_limit_bytes=60 << 20),
        cost_estimate=pl.CostEstimate(flops=flops, bytes_accessed=moved, transcendentals=0),
        name=name,
    )(*far, *near)


def exchange(v):
    return lax.all_to_all(v, "seq", split_axis=0, concat_axis=0, tiled=True)


def on_device(seq, inputs, norm_gain, inner_factor, outer_factor, twiddle, channel_weight, cotangent):
    rows, n2, width = inputs.shape
    s = Sizes(seq, rows, n2, width)
    full = s.block + s.extra
    rows_bf16 = (inputs.shape, BF16)
    square = ((n2, n2), BF16)
    packed = ((seq, s.block, LANES), BF16)
    packed_more = ((seq, full, LANES), BF16)
    wide = ((seq * s.block, LANES), F32)
    small = ((rows, n2), F32)
    mib = rows * n2 * width * 2
    flop = 2 * rows * n2 * n2 * width
    gain = norm_gain.reshape(1, width)

    (part_sum,) = call(square_kernel, s, "squares", [small], [rows_bf16], rows, flop // 20, mib, [inputs], [])
    sq_sum = lax.psum(part_sum, "chan")
    send, inv = call(
        inner_kernel, s, "inner", [((seq, 2 * s.block, LANES), BF16), small],
        [rows_bf16, rows_bf16, square, wide, wide, packed, packed], 2 * rows + 2 + CHUNKS, flop, 5 * mib,
        [inputs, cotangent, inner_factor], [sq_sum, gain, twiddle],
    )
    got = exchange(send)
    (back_send,) = call(
        middle_kernel, s, "middle", [packed_more],
        [
            ((4, seq, s.block // 2, LANES), BF16), (outer_factor.shape, BF16), ((s.parts * width, LANES), F32),
            ((seq // 2, 2, full // 8, 8, LANES), F32), packed_more,
        ],
        5 + CHUNKS, 3 * flop, 4 * mib, [got, outer_factor], [channel_weight[0]],
    )
    back_got = exchange(back_send)
    pairs = jnp.sum(back_got[:, s.block :].astype(F32), axis=0)
    share = pairs[: s.extra // 2] + pairs[s.extra // 2 :]
    whole = exchange(jnp.broadcast_to(share, (seq,) + share.shape))
    base, part_proj = call(
        back_kernel, s, "back", [(inputs.shape, F32), small],
        [packed_more, rows_bf16, rows_bf16, square, (inputs.shape, F32), ((seq * full, LANES), F32), ((n2, width), BF16)],
        CHUNKS + 1 + 3 * rows, flop, 6 * mib, [back_got, inputs, cotangent, inner_factor], [inv, gain, twiddle],
    )
    projection = lax.psum(part_proj, "chan")
    input_grad, weight_grad = call(
        finish_kernel, s, "finish", [rows_bf16, ((width, width), F32)],
        [(inputs.shape, F32), rows_bf16, rows_bf16], 3 * rows, flop // 100, 4 * mib,
        [base, inputs], [inv, projection, whole.reshape(-1, LANES)],
    )
    return (input_grad, weight_grad.reshape(1, width, width))


def solution(mesh):
    in_specs = (
        P("seq", None, "chan"),
        P("chan"),
        P(),
        P(),
        P("seq", None),
        P("chan", None, None),
        P("seq", None, "chan"),
    )
    out_specs = (P("seq", None, "chan"), P("chan", None, None))

    def run(*args):
        return on_device(mesh.shape["seq"], *args)

    return jax.shard_map(run, mesh=mesh, in_specs=in_specs, out_specs=out_specs, check_vma=False)
```

time: 171 us -> 177 us (1.035)
  Pallas kernels: 25.5 us -> 30.8 us
    pallas_call x5, Pallas kernels: 25.5 us -> 30.8 us  [call(): pl.pallas_call(functools.partial(kernel, s), out_shape=[jax.ShapeDtypeStr...]
where the time goes in v3:
time: 177 us; the launch traced here: 175 us
  blocking collectives  135 us (76%)
  Pallas kernels  30.8 us (17%)
  starting transfers between devices  6.9 us (4%)
    all_to_all x2, blocking collectives, exchange(): return lax.all_to_all(v, 'seq', split_axis=0, concat_axis=0, tiled=True)  107 us
    pallas_call x5, Pallas kernels, call(): pl.pallas_call(functools.partial(kernel, s), out_shape=[jax.ShapeDtypeStr...  30.8 us
    psum x1, blocking collectives, on_device(): sq_sum = lax.psum(part_sum, 'chan')  16.6 us
    psum x1, blocking collectives, on_device(): projection = lax.psum(part_proj, 'chan')  11.1 us
    all_to_all x1, starting transfers between devices, exchange(): return lax.all_to_all(v, 'seq', split_axis=0, concat_axis=0, tiled=True)  6.9 us
  transfers between devices with their start and end apart: 1, of which 0 were waited for; matrix products, arithmetic and copies ran while one was open for 0% of the time, Pallas kernels for 4%

profile of v3, /device:TPU:1, one launch (start us, length us, event | category | flops | bytes accessed | tf_op | source)
XLA Modules:
  0.0 175.1 jit_solution(2303802037231717148)
XLA Ops:
  0.6 2.7 %squares.1 = f32[4,512]{1,0:T(4,128)} custom-call(bf16[4,512,256]{2,1,0:T(8,128)(2,1)} %x_hbm.7), custom_call_target="tpu_custom_call" | custom-call | flops 26843544 | bytes 1048576 | tf_op jit(solution)/shard_map/squares/pallas_call | solution.py:246
  3.3 16.6 %psum.14.sum_ref = f32[4,512]{1,0:T(4,128)} all-reduce(f32[4,512]{1,0:T(4,128)} %squares.1), channel_id=1, replica_groups=mesh['seq'=128,'chan'=4] {'chan'}, use_global_device_ids=true, to_apply=%region_0.0 | all-reduce | flops 2048 | bytes 16384 | tf_op jit(solution)/shard_map/psum | solution.py:278
  19.9 8.7 %inner.1 = (bf16[128,64,128]{2,1,0:T(8,128)(2,1)}, f32[4,512]{1,0:T(4,128)}) custom-call(bf16[4,512,256]{2,1,0:T(8,128)(2,1)} %x_hbm.7, bf16[4,512,256]{2,1,0:T(8,128)(2,1)} %cot_hbm.3, bf16[512,512]{1,0:T(8,128)(2,1)} %inner_hbm.3, f32[4,512]{1,0:T(4,128)} %psum.14.sum_ref, f32[1,256]{1,0:T(1,128)} %bitcast.5, f32[4,512]{1,0:T(4,128)} %tw_ref.3), custom_call_target="tpu_custom_call" | custom-call | flops 536870912 | bytes 5242880 | tf_op jit(solution)/shard_map/inner/pallas_call | solution.py:246
  28.6 63.8 %all_to_all.15.got_hbm = bf16[128,64,128]{2,1,0:T(8,128)(2,1)} all-to-all(bf16[128,64,128]{2,1,0:T(8,128)(2,1)} %get-tuple-element.8), channel_id=1, replica_groups=mesh['seq'=128,'chan'=4] {'seq'}, dimensions={0} | all-to-all | bytes 4194304 | tf_op jit(solution)/shard_map/all_to_all | solution.py:260
  92.5 7.1 %middle.1 = bf16[128,40,128]{2,1,0:T(8,128)(2,1)} custom-call(bf16[128,64,128]{2,1,0:T(8,128)(2,1)} %all_to_all.15.got_hbm, bf16[512,512]{1,0:T(8,128)(2,1)} %outer_hbm.1, bf16[256,256]{1,0:T(8,128)(2,1)} %bitcast.8), custom_call_target="tpu_custom_call" | custom-call | flops 1610612736 | bytes 4194304 | tf_op jit(solution)/shard_map/middle/pallas_call | solution.py:246
  99.6 43.2 %all_to_all.16.got_hbm = bf16[128,40,128]{2,1,0:T(8,128)(2,1)S(1)} all-to-all(bf16[128,40,128]{2,1,0:T(8,128)(2,1)} %middle.1), channel_id=1, replica_groups=mesh['seq'=128,'chan'=4] {'seq'}, dimensions={0} | all-to-all | bytes 2621440 | tf_op jit(solution)/shard_map/all_to_all | solution.py:260
  142.8 0.0 copy-start
  142.8 0.1 convert_reduce_fusion
  143.0 0.9 broadcast_in_dim.3
  143.9 6.9 %all-to-all-start.2 = ((f32[128,4,128]{2,1,0:T(4,128)}), f32[128,4,128]{2,1,0:T(4,128)S(1)}, u32[]{:S(2)}, u32[]{:S(2)}) async-start(f32[128,4,128]{2,1,0:T(4,128)} %broadcast_in_dim.3), calls=%async_computation.2 | async-start | bytes 524288 | tf_op jit(solution)/shard_map/all_to_all | solution.py:260
  150.8 0.0 copy-done
  150.8 7.8 %back.1 = (f32[4,512,256]{2,1,0:T(8,128)}, f32[4,512]{1,0:T(4,128)}) custom-call(bf16[128,40,128]{2,1,0:T(8,128)(2,1)} %copy-done, bf16[4,512,256]{2,1,0:T(8,128)(2,1)} %x_hbm.7, bf16[4,512,256]{2,1,0:T(8,128)(2,1)} %cot_hbm.3, bf16[512,512]{1,0:T(8,128)(2,1)} %inner_hbm.3, f32[4,512]{1,0:T(4,128)} %get-tuple-element.9.inv_ref, f32[1,256]{1,0:T(1,128)} %bitcast.6, ...), custom_call_target="tpu_custom_call" | custom-call | flops 536870912 | bytes 6291456 | tf_op jit(solution)/shard_map/back/pallas_call | solution.py:246
  158.6 11.1 %psum.15.proj_ref = f32[4,512]{1,0:T(4,128)} all-reduce(f32[4,512]{1,0:T(4,128)} %get-tuple-element.11), channel_id=1, replica_groups=mesh['seq'=128,'chan'=4] {'chan'}, use_global_device_ids=true, to_apply=%region_1.0 | all-reduce | flops 2048 | bytes 16384 | tf_op jit(solution)/shard_map/psum | solution.py:302
  169.7 0.0 all-to-all-done.2
  169.7 0.0 copy-start.1
  169.7 0.7 copy-done.1
  170.5 4.4 %finish.1 = (bf16[4,512,256]{2,1,0:T(8,128)(2,1)}, f32[256,256]{1,0:T(8,128)}) custom-call(f32[4,512,256]{2,1,0:T(8,128)} %get-tuple-element.10.sum_hbm, bf16[4,512,256]{2,1,0:T(8,128)(2,1)} %x_hbm.7, f32[4,512]{1,0:T(4,128)} %get-tuple-element.9.inv_ref, f32[4,512]{1,0:T(4,128)} %psum.15.proj_ref, f32[512,128]{1,0:T(8,128)} %bitcast.4), custom_call_target="tpu_custom_call" | custom-call | flops 5368709 | bytes 4194304 | tf_op jit(solution)/shard_map/finish/pallas_call | solution.py:246
  (1 shorter events, 0.0 us)
Async XLA Ops:
  142.8 8.0 %copy-start = (bf16[128,40,128]{2,1,0:T(8,128)(2,1)}, bf16[128,40,128]{2,1,0:T(8,128)(2,1)S(1)}, u32[]{:S(2)}) copy-start(bf16[128,40,128]{2,1,0:T(8,128)(2,1)S(1)} %all_to_all.16.got_hbm) | copy-start | bytes 3932164
  143.9 25.9 %all-to-all-start.2 = ((f32[128,4,128]{2,1,0:T(4,128)}), f32[128,4,128]{2,1,0:T(4,128)S(1)}, u32[]{:S(2)}, u32[]{:S(2)}) async-start(f32[128,4,128]{2,1,0:T(4,128)} %broadcast_in_dim.3), calls=%async_computation.2 | async-start | bytes 524288 | tf_op jit(solution)/shard_map/all_to_all | solution.py:260
  169.7 0.7 copy-start.1

commit v4 on v2

--- a/solution.py
+++ b/solution.py
@@ -45,25 +45,59 @@
                 yield jh, part, (jh * self.parts + part) * self.rows
 
 
+class Copies:
+    def __init__(self, sems):
+        self.sems, self.count = sems, 0
+
+    def start(self, source, target):
+        copy = pltpu.make_async_copy(source, target, self.sems.at[self.count])
+        copy.start()
+        self.count += 1
+        return copy
+
+    def rows(self, source, target, count):
+        return [self.start(source.at[r], target.at[r]) for r in range(count)]
+
+
+def wait(copies):
+    for copy in copies:
+        copy.wait()
+
+
 def square_kernel(s, x_ref, sum_ref):
     for r in range(s.rows):
         x = x_ref[r].astype(F32)
         sum_ref[r : r + 1, :] = lane_sums(x * x)[0:1]
 
 
-def inner_kernel(s, x_ref, cot_ref, sum_ref, gain_ref, inner_ref, tw_ref, send_ref, inv_ref, wide_ref):
+def inner_kernel(
+    s, cot_hbm, inner_hbm, x_hbm, gain_hbm, tw_hbm, sum_ref, send_ref, inv_ref,
+    cot_ref, inner_ref, x_ref, gain_ref, tw_ref, wide_ref, sems,
+):
+    copies = Copies(sems)
+    cot_load = copies.start(cot_hbm, cot_ref)
+    tw_load = copies.start(tw_hbm, tw_ref)
+    gain_load = copies.start(gain_hbm, gain_ref)
+    inner_load = copies.start(inner_hbm, inner_ref)
+    x_load = copies.start(x_hbm, x_ref)
     inv = lax.rsqrt(sum_ref[...] / D + 1e-05)
     inv_ref[...] = inv
     inv_cols = column_form(inv)
+    cot_load.wait()
+    for r in range(s.rows):
+        for jh, part, q in s.pieces():
+            wide_ref[pl.ds(s.block + q + r, s.seq, 2 * s.block), :] = cot_ref[
+                r, jh * s.seq : (jh + 1) * s.seq, part * LANES : (part + 1) * LANES
+            ].astype(F32)
+    wait([tw_load, gain_load, inner_load, x_load])
     tw_cols = column_form(tw_ref[...])
     for r in range(s.rows):
         normed = (x_ref[r].astype(F32) * inv_cols[:, r : r + 1] * gain_ref[...]).astype(BF16)
         y = dot(inner_ref[...], normed, 1, 0) * tw_cols[:, r : r + 1]
-        cot = cot_ref[r].astype(F32)
         for jh, part, q in s.pieces():
-            here = slice(jh * s.seq, (jh + 1) * s.seq), slice(part * LANES, (part + 1) * LANES)
-            wide_ref[pl.ds(q + r, s.seq, 2 * s.block), :] = y[here]
-            wide_ref[pl.ds(s.block + q + r, s.seq, 2 * s.block), :] = cot[here]
+            wide_ref[pl.ds(q + r, s.seq, 2 * s.block), :] = y[
+                jh * s.seq : (jh + 1) * s.seq, part * LANES : (part + 1) * LANES
+            ]
     send_ref[...] = wide_ref[...].astype(BF16)
 
 
@@ -124,8 +158,12 @@
     send_ref[...] = flat[...].astype(BF16)
 
 
-def back_kernel(s, got_ref, x_ref, cot_ref, inv_ref, gain_ref, tw_ref, inner_ref, sum_ref, proj_ref, wide_ref, col_ref):
-    inner_t = dot(unit(s.n2), inner_ref[...], 1, 1).astype(BF16)
+def back_kernel(
+    s, inner_hbm, got_ref, x_ref, cot_ref, inv_ref, gain_ref, tw_ref, sum_hbm, proj_ref,
+    inner_ref, sum_ref, wide_ref, col_ref, sems,
+):
+    copies = Copies(sems)
+    load = copies.start(inner_hbm, inner_ref)
     wide_ref[...] = got_ref[...].astype(F32)
     full = s.block + s.extra
     inv_cols = column_form(inv_ref[...])
@@ -133,33 +171,62 @@
     for r in range(s.rows):
         for jh, part, q in s.pieces():
             here = slice(jh * s.seq, (jh + 1) * s.seq)
-            col_ref[here, part * LANES : (part + 1) * LANES] = (
+            col_ref[r, here, part * LANES : (part + 1) * LANES] = (
                 wide_ref[pl.ds(q + r, s.seq, full), :] * tw_cols[here, r : r + 1]
             ).astype(BF16)
-        grad = dot(inner_t, col_ref[...], 1, 0)
+    load.wait()
+    inner_t = dot(unit(s.n2), inner_ref[...], 1, 1).astype(BF16)
+    stores = []
+    for r in range(s.rows):
+        grad = dot(inner_t, col_ref[r], 1, 0)
         gained = grad * gain_ref[...]
         proj_ref[r : r + 1, :] = lane_sums(gained * x_ref[r].astype(F32))[0:1]
         sum_ref[r] = cot_ref[r].astype(F32) + inv_cols[:, r : r + 1] * gained
-
-
-def finish_kernel(s, sum_ref, x_ref, inv_ref, proj_ref, whole_ref, out_ref, weight_ref):
+        if r % 2 == 1:
+            stores.append(copies.start(sum_ref.at[r - 1 : r + 1], sum_hbm.at[r - 1 : r + 1]))
+    wait(stores)
+
+
+def finish_kernel(
+    s, sum_hbm, whole_hbm, x_ref, inv_ref, proj_ref, out_hbm, weight_hbm, sum_ref, whole_ref, weight_ref, out_ref, sems
+):
+    copies = Copies(sems)
+    pairs = [slice(r, r + 2) for r in range(0, s.rows, 2)]
+    sum_loads = [copies.start(sum_hbm.at[pair], sum_ref.at[pair]) for pair in pairs]
+    whole_load = copies.start(whole_hbm, whole_ref)
+    inv = inv_ref[...]
+    factor = column_form(inv * inv * inv * proj_ref[...] / D)
+    stores = []
+    for k, pair in enumerate(pairs):
+        sum_loads[k].wait()
+        for r in (2 * k, 2 * k + 1):
+            out_ref[r] = (sum_ref[r] - x_ref[r].astype(F32) * factor[:, r : r + 1]).astype(BF16)
+        stores.append(copies.start(out_ref.at[pair], out_hbm.at[pair]))
+    whole_load.wait()
     for part in range(s.parts):
         weight_ref[:, part * LANES : (part + 1) * LANES] = whole_ref[pl.ds(part, s.width, s.parts), :]
-    inv = inv_ref[...]
-    factor = column_form(inv * inv * inv * proj_ref[...] / D)
-    for r in range(s.rows):
-        out_ref[r] = (sum_ref[r] - x_ref[r].astype(F32) * factor[:, r : r + 1]).astype(BF16)
-
-
-def call(kernel, s, name, outs, scratch, flops, moved, *args):
+    stores.append(copies.start(weight_ref, weight_hbm))
+    wait(stores)
+
+
+HBM, AUTO = "hbm", "auto"
+
+
+def call(kernel, s, name, outs, scratch, copies, flops, moved, *args):
+    specs = {AUTO: pl.BlockSpec(memory_space=pltpu.VMEM), HBM: pl.BlockSpec(memory_space=pl.ANY)}
     return pl.pallas_call(
         functools.partial(kernel, s),
-        out_shape=[jax.ShapeDtypeStruct(shape, kind) for shape, kind in outs],
-        scratch_shapes=[pltpu.VMEM(shape, kind) for shape, kind in scratch],
-        compiler_params=pltpu.CompilerParams(vmem_limit_bytes=60 << 20),
+        out_shape=[
+            (pltpu.HBM if place == HBM else jax.ShapeDtypeStruct)(shape, kind) for shape, kind, place in outs
+        ],
+        in_specs=[specs[place] for _, place in args],
+        out_specs=[specs[place] for _, _, place in outs],
+        scratch_shapes=[pltpu.VMEM(shape, kind) for shape, kind in scratch]
+        + ([pltpu.SemaphoreType.DMA((copies,))] if copies else []),
+        compiler_params=pltpu.CompilerParams(vmem_limit_bytes=24 << 20),
         cost_estimate=pl.CostEstimate(flops=flops, bytes_accessed=moved, transcendentals=0),
         name=name,
-    )(*args)
+    )(*[pltpu.with_memory_space_constraint(v, pltpu.HBM) if place == HBM else v for v, place in args])
 
 
 def exchange(v, seq):
@@ -175,18 +242,23 @@
     mib = rows * n2 * width * 2
     flop = 2 * rows * n2 * n2 * width
     gain = norm_gain.reshape(1, width)
-    weight = channel_weight[0]
-    (part_sum,) = call(square_kernel, s, "squares", [((rows, n2), F32)], [], flop // 20, mib, inputs)
+    small = (rows, n2)
+
+    (part_sum,) = call(
+        square_kernel, s, "squares", [(small, F32, AUTO)], [], 0, flop // 20, mib, (inputs, AUTO)
+    )
     sq_sum = lax.psum(part_sum, "chan")
     send, inv = call(
-        inner_kernel, s, "inner", [(packed_two, BF16), ((rows, n2), F32)], [(packed_two, F32)], flop, 5 * mib,
-        inputs, cotangent, sq_sum, gain, inner_factor, twiddle,
+        inner_kernel, s, "inner", [(packed_two, BF16, AUTO), (small, F32, AUTO)],
+        [(inputs.shape, BF16), (inner_factor.shape, BF16), (inputs.shape, BF16), (gain.shape, F32), (small, F32), (packed_two, F32)],
+        5, flop, 5 * mib,
+        (cotangent, HBM), (inner_factor, HBM), (inputs, HBM), (gain, HBM), (twiddle, HBM), (sq_sum, AUTO),
     )
     got = exchange(send, seq)
     (back_send,) = call(
-        middle_kernel, s, "middle", [(packed_more, BF16)],
-        [((s.parts * width, LANES), F32), ((seq // 2, 2, (s.block + s.extra) // 8, 8, LANES), F32)], 3 * flop, 4 * mib,
-        got, weight, outer_factor,
+        middle_kernel, s, "middle", [(packed_more, BF16, AUTO)],
+        [((s.parts * width, LANES), F32), ((seq // 2, 2, (s.block + s.extra) // 8, 8, LANES), F32)], 0, 3 * flop, 4 * mib,
+        (got, AUTO), (channel_weight[0], AUTO), (outer_factor, AUTO),
     )
     back_got = exchange(back_send, seq)
     pairs = back_got.reshape(seq, s.block + s.extra, LANES)[:, s.block :].astype(F32)
@@ -196,14 +268,16 @@
         jnp.broadcast_to(share, (seq,) + share.shape), "seq", split_axis=0, concat_axis=0, tiled=True
     )
     base, part_proj = call(
-        back_kernel, s, "back", [(inputs.shape, F32), ((rows, n2), F32)],
-        [(packed_more, F32), ((n2, width), BF16)], flop, 6 * mib,
-        back_got, inputs, cotangent, inv, gain, twiddle, inner_factor,
+        back_kernel, s, "back", [(inputs.shape, F32, HBM), (small, F32, AUTO)],
+        [(inner_factor.shape, BF16), (inputs.shape, F32), (packed_more, F32), (inputs.shape, BF16)], 1 + rows // 2, flop, 6 * mib,
+        (inner_factor, HBM), (back_got, AUTO), (inputs, AUTO), (cotangent, AUTO), (inv, AUTO), (gain, AUTO), (twiddle, AUTO),
     )
     projection = lax.psum(part_proj, "chan")
     input_grad, weight_grad = call(
-        finish_kernel, s, "finish", [(inputs.shape, BF16), ((width, width), F32)], [], flop // 100, 4 * mib,
-        base, inputs, inv, projection, whole.reshape(-1, LANES),
+        finish_kernel, s, "finish", [(inputs.shape, BF16, HBM), ((width, width), F32, HBM)],
+        [(inputs.shape, F32), ((s.parts * width, LANES), F32), ((width, width), F32), (inputs.shape, BF16)],
+        rows + 2, flop // 100, 4 * mib,
+        (base, HBM), (whole.reshape(-1, LANES), HBM), (inputs, AUTO), (inv, AUTO), (projection, AUTO),
     )
     return (input_grad, weight_grad.reshape(1, width, width))
 

time: 171 us -> 163 us (0.953)
  Pallas kernels: 25.5 us -> 17.8 us
  blocking collectives: 135 us -> 133 us
    pallas_call x5, Pallas kernels: 25.5 us -> 17.8 us  [call(): pl.pallas_call(functools.partial(kernel, s), out_shape=[(pltpu.HBM if pla...]
  transfers between devices with their start and end apart: 1 -> 1, of which waited for: 0 -> 0; matrix products, arithmetic and copies ran while one was open for 0% -> 0% of each run, Pallas kernels for 4% -> 3%
where the time goes in v4:
time: 163 us; the launch traced here: 162 us
  blocking collectives  133 us (82%)
  Pallas kernels  17.8 us (11%)
  starting transfers between devices  7.96 us (5%)
  local copies, waits for them, and re-layouts  2 us (1%)
    all_to_all x2, blocking collectives, exchange(): lax.all_to_all(packed, 'seq', split_axis=0, concat_axis=0, tiled=True)  107 us
    pallas_call x5, Pallas kernels, call(): pl.pallas_call(functools.partial(kernel, s), out_shape=[(pltpu.HBM if pla...  17.8 us
    psum x1, blocking collectives, on_device(): sq_sum = lax.psum(part_sum, 'chan')  15.9 us
    psum x1, blocking collectives, on_device(): projection = lax.psum(part_proj, 'chan')  10.5 us
    all_to_all x1, starting transfers between devices, on_device(): lax.all_to_all(jnp.broadcast_to(share, (seq,) + share.shape), 'seq', spli...  7.96 us
  transfers between devices with their start and end apart: 1, of which 0 were waited for; matrix products, arithmetic and copies ran while one was open for 0% of the time, Pallas kernels for 3%

profile of v4, /device:TPU:1, one launch (start us, length us, event | category | flops | bytes accessed | tf_op | source)
XLA Modules:
  0.0 162.0 jit_solution(3192464336437056394)
XLA Ops:
  0.6 0.0 copy-start
  0.6 1.2 copy-done
  1.9 0.7 squares.1
  2.5 15.9 %psum.14.sum_ref = f32[4,512]{1,0:T(4,128)S(1)} all-reduce(f32[4,512]{1,0:T(4,128)S(1)} %squares.1), channel_id=1, replica_groups=mesh['seq'=128,'chan'=4] {'chan'}, use_global_device_ids=true, to_apply=%region_0.0 | all-reduce | flops 2048 | bytes 16384 | tf_op jit(solution)/shard_map/psum | solution.py:250
  18.4 5.8 %inner.1 = (bf16[8192,128]{1,0:T(8,128)(2,1)S(1)}, f32[4,512]{1,0:T(4,128)S(1)}) custom-call(bf16[4,512,256]{2,1,0:T(8,128)(2,1)} %cot_ref.1, bf16[512,512]{1,0:T(8,128)(2,1)} %inner_hbm.3, bf16[4,512,256]{2,1,0:T(8,128)(2,1)} %x_ref.5, f32[1,256]{1,0:T(1,128)} %bitcast.12, f32[4,512]{1,0:T(4,128)} %tw_ref.1, f32[4,512]{1,0:T(4,128)S(1)} %psum.14.sum_ref), custom_call_target="tpu_custom_call" | custom-call | flops 536870912 | bytes 5242880 | tf_op jit(solution)/shard_map/inner/pallas_call | solution.py:217
  24.2 0.0 copy-start.5
  24.2 0.0 copy-start.6
  24.2 63.7 %all_to_all.15 = bf16[128,64,128]{2,1,0:T(8,128)(2,1)S(1)} all-to-all(bf16[128,64,128]{2,1,0:T(8,128)(2,1)S(1)} %bitcast.9), channel_id=1, replica_groups=mesh['seq'=128,'chan'=4] {'seq'}, dimensions={0} | all-to-all | bytes 4194304 | tf_op jit(solution)/shard_map/all_to_all | solution.py:234
  87.9 0.0 copy-done.5
  87.9 0.0 copy-done.6
  87.9 3.6 %middle.1 = bf16[5120,128]{1,0:T(8,128)(2,1)S(1)} custom-call(bf16[8192,128]{1,0:T(8,128)(2,1)S(1)} %bitcast.10, bf16[256,256]{1,0:T(8,128)(2,1)S(1)} %bitcast.14, bf16[512,512]{1,0:T(8,128)(2,1)S(1)} %copy-done.5), custom_call_target="tpu_custom_call" | custom-call | flops 1610612736 | bytes 4194304 | tf_op jit(solution)/shard_map/middle/pallas_call | solution.py:217
  91.4 0.0 copy-start.1
  91.5 0.0 copy-start.2
  91.5 0.0 copy-start.3
  91.5 0.0 copy-start.4
  91.5 43.2 %all_to_all.16 = bf16[128,40,128]{2,1,0:T(8,128)(2,1)S(1)} all-to-all(bf16[128,40,128]{2,1,0:T(8,128)(2,1)S(1)} %bitcast.11), channel_id=1, replica_groups=mesh['seq'=128,'chan'=4] {'seq'}, dimensions={0} | all-to-all | bytes 2621440 | tf_op jit(solution)/shard_map/all_to_all | solution.py:234
  134.7 0.1 convert_reduce_fusion
  134.8 0.7 broadcast_in_dim.3
  135.5 8.0 %all-to-all-start.2 = ((f32[128,4,128]{2,1,0:T(4,128)}), f32[128,4,128]{2,1,0:T(4,128)}, u32[]{:S(2)}, u32[]{:S(2)}) async-start(f32[128,4,128]{2,1,0:T(4,128)} %broadcast_in_dim.3), calls=%async_computation.2 | async-start | bytes 524288 | tf_op jit(solution)/shard_map/all_to_all | solution.py:267
  143.5 0.0 copy-done.1
  143.5 5.1 %back.1 = (f32[4,512,256]{2,1,0:T(8,128)}, f32[4,512]{1,0:T(4,128)S(1)}) custom-call(bf16[512,512]{1,0:T(8,128)(2,1)} %inner_hbm.3, bf16[5120,128]{1,0:T(8,128)(2,1)S(1)} %bitcast.8, bf16[4,512,256]{2,1,0:T(8,128)(2,1)S(1)} %copy-done.1, bf16[4,512,256]{2,1,0:T(8,128)(2,1)S(1)} %copy-done.2, f32[4,512]{1,0:T(4,128)S(1)} %get-tuple-element.9.inv_ref, ...), custom_call_target="tpu_custom_call" | custom-call | flops 536870912 | bytes 6291456 | tf_op jit(solution)/shard_map/back/pallas_call | solution.py:217
  148.7 10.5 %psum.15.proj_ref = f32[4,512]{1,0:T(4,128)S(1)} all-reduce(f32[4,512]{1,0:T(4,128)S(1)} %get-tuple-element.11), channel_id=1, replica_groups=mesh['seq'=128,'chan'=4] {'chan'}, use_global_device_ids=true, to_apply=%region_2.0 | all-reduce | flops 2048 | bytes 16384 | tf_op jit(solution)/shard_map/psum | solution.py:275
  159.2 0.0 all-to-all-done.2
  159.2 2.7 %finish.1 = (bf16[4,512,256]{2,1,0:T(8,128)(2,1)}, f32[256,256]{1,0:T(8,128)}) custom-call(f32[4,512,256]{2,1,0:T(8,128)} %get-tuple-element.10.sum_hbm, f32[512,128]{1,0:T(8,128)} %bitcast.6.whole_hbm, bf16[4,512,256]{2,1,0:T(8,128)(2,1)S(1)} %copy-done.1, f32[4,512]{1,0:T(4,128)S(1)} %get-tuple-element.9.inv_ref, f32[4,512]{1,0:T(4,128)S(1)} %psum.15.proj_ref), custom_call_target="tpu_custom_call" | custom-call | flops 5368709 | bytes 4194304 | tf_op jit(solution)/shard_map/finish/pallas_call | solution.py:217
  (4 shorter events, 0.0 us)
Async XLA Ops:
  0.6 1.2 copy-start
  24.2 63.7 %copy-start.5 = (bf16[512,512]{1,0:T(8,128)(2,1)S(1)}, bf16[512,512]{1,0:T(8,128)(2,1)}, u32[]{:S(2)}) copy-start(bf16[512,512]{1,0:T(8,128)(2,1)} %outer_ref.1) | copy-start | bytes 1572868
  24.2 63.7 %copy-start.6 = (bf16[1,256,256]{2,1,0:T(8,128)(2,1)S(1)}, bf16[1,256,256]{2,1,0:T(8,128)(2,1)}, u32[]{:S(2)}) copy-start(bf16[1,256,256]{2,1,0:T(8,128)(2,1)} %param.12) | copy-start | bytes 393220
  91.4 52.1 %copy-start.1 = (bf16[4,512,256]{2,1,0:T(8,128)(2,1)S(1)}, bf16[4,512,256]{2,1,0:T(8,128)(2,1)}, u32[]{:S(2)}) copy-start(bf16[4,512,256]{2,1,0:T(8,128)(2,1)} %x_ref.5) | copy-start | bytes 3145732
  91.5 52.1 %copy-start.2 = (bf16[4,512,256]{2,1,0:T(8,128)(2,1)S(1)}, bf16[4,512,256]{2,1,0:T(8,128)(2,1)}, u32[]{:S(2)}) copy-start(bf16[4,512,256]{2,1,0:T(8,128)(2,1)} %cot_ref.1) | copy-start | bytes 3145732
  91.5 52.1 %copy-start.3 = (f32[4,512]{1,0:T(4,128)S(1)}, f32[4,512]{1,0:T(4,128)}, u32[]{:S(2)}) copy-start(f32[4,512]{1,0:T(4,128)} %tw_ref.1) | copy-start | bytes 24580
  91.5 52.1 %copy-start.4 = (f32[256]{0:T(256)S(1)}, f32[256]{0:T(256)}, u32[]{:S(2)}) copy-start(f32[256]{0:T(256)} %param.8) | copy-start | bytes 3076
  135.5 23.6 %all-to-all-start.2 = ((f32[128,4,128]{2,1,0:T(4,128)}), f32[128,4,128]{2,1,0:T(4,128)}, u32[]{:S(2)}, u32[]{:S(2)}) async-start(f32[128,4,128]{2,1,0:T(4,128)} %broadcast_in_dim.3), calls=%async_computation.2 | async-start | bytes 524288 | tf_op jit(solution)/shard_map/all_to_all | solution.py:267

commit v5 on v4

--- a/solution.py
+++ b/solution.py
@@ -45,6 +45,13 @@
                 yield jh, part, (jh * self.parts + part) * self.rows
 
 
+def total(ref):
+    terms = [ref[k] for k in range(ref.shape[0])]
+    while len(terms) > 1:
+        terms = [a + b for a, b in zip(terms[::2], terms[1::2])]
+    return terms[0]
+
+
 class Copies:
     def __init__(self, sems):
         self.sems, self.count = sems, 0
@@ -75,16 +82,18 @@
     cot_ref, inner_ref, x_ref, gain_ref, tw_ref, wide_ref, sems,
 ):
     copies = Copies(sems)
-    cot_load = copies.start(cot_hbm, cot_ref)
+    pairs = [slice(r, r + 2) for r in range(0, s.rows, 2)]
+    cot_loads = [copies.start(cot_hbm.at[pair], cot_ref.at[pair]) for pair in pairs]
     tw_load = copies.start(tw_hbm, tw_ref)
     gain_load = copies.start(gain_hbm, gain_ref)
     inner_load = copies.start(inner_hbm, inner_ref)
     x_load = copies.start(x_hbm, x_ref)
-    inv = lax.rsqrt(sum_ref[...] / D + 1e-05)
+    inv = lax.rsqrt(total(sum_ref) / D + 1e-05)
     inv_ref[...] = inv
     inv_cols = column_form(inv)
-    cot_load.wait()
-    for r in range(s.rows):
+    for r in range(s.rows):
+        if r % 2 == 0:
+            cot_loads[r // 2].wait()
         for jh, part, q in s.pieces():
             wide_ref[pl.ds(s.block + q + r, s.seq, 2 * s.block), :] = cot_ref[
                 r, jh * s.seq : (jh + 1) * s.seq, part * LANES : (part + 1) * LANES
@@ -182,8 +191,7 @@
         gained = grad * gain_ref[...]
         proj_ref[r : r + 1, :] = lane_sums(gained * x_ref[r].astype(F32))[0:1]
         sum_ref[r] = cot_ref[r].astype(F32) + inv_cols[:, r : r + 1] * gained
-        if r % 2 == 1:
-            stores.append(copies.start(sum_ref.at[r - 1 : r + 1], sum_hbm.at[r - 1 : r + 1]))
+        stores.append(copies.start(sum_ref.at[r], sum_hbm.at[r]))
     wait(stores)
 
 
@@ -191,17 +199,16 @@
     s, sum_hbm, whole_hbm, x_ref, inv_ref, proj_ref, out_hbm, weight_hbm, sum_ref, whole_ref, weight_ref, out_ref, sems
 ):
     copies = Copies(sems)
-    pairs = [slice(r, r + 2) for r in range(0, s.rows, 2)]
-    sum_loads = [copies.start(sum_hbm.at[pair], sum_ref.at[pair]) for pair in pairs]
+    sum_loads = [copies.start(sum_hbm.at[r], sum_ref.at[r]) for r in range(s.rows)]
     whole_load = copies.start(whole_hbm, whole_ref)
     inv = inv_ref[...]
-    factor = column_form(inv * inv * inv * proj_ref[...] / D)
+    factor = column_form(inv * inv * inv * total(proj_ref) / D)
     stores = []
-    for k, pair in enumerate(pairs):
-        sum_loads[k].wait()
-        for r in (2 * k, 2 * k + 1):
-            out_ref[r] = (sum_ref[r] - x_ref[r].astype(F32) * factor[:, r : r + 1]).astype(BF16)
-        stores.append(copies.start(out_ref.at[pair], out_hbm.at[pair]))
+    for r in range(s.rows):
+        sum_loads[r].wait()
+        out_ref[r] = (sum_ref[r] - x_ref[r].astype(F32) * factor[:, r : r + 1]).astype(BF16)
+        if r % 2 == 1:
+            stores.append(copies.start(out_ref.at[r - 1 : r + 1], out_hbm.at[r - 1 : r + 1]))
     whole_load.wait()
     for part in range(s.parts):
         weight_ref[:, part * LANES : (part + 1) * LANES] = whole_ref[pl.ds(part, s.width, s.parts), :]
@@ -247,12 +254,12 @@
     (part_sum,) = call(
         square_kernel, s, "squares", [(small, F32, AUTO)], [], 0, flop // 20, mib, (inputs, AUTO)
     )
-    sq_sum = lax.psum(part_sum, "chan")
+    sums = lax.all_gather(part_sum, "chan")
     send, inv = call(
         inner_kernel, s, "inner", [(packed_two, BF16, AUTO), (small, F32, AUTO)],
         [(inputs.shape, BF16), (inner_factor.shape, BF16), (inputs.shape, BF16), (gain.shape, F32), (small, F32), (packed_two, F32)],
-        5, flop, 5 * mib,
-        (cotangent, HBM), (inner_factor, HBM), (inputs, HBM), (gain, HBM), (twiddle, HBM), (sq_sum, AUTO),
+        4 + rows // 2, flop, 5 * mib,
+        (cotangent, HBM), (inner_factor, HBM), (inputs, HBM), (gain, HBM), (twiddle, HBM), (sums, AUTO),
     )
     got = exchange(send, seq)
     (back_send,) = call(
@@ -269,15 +276,15 @@
     )
     base, part_proj = call(
         back_kernel, s, "back", [(inputs.shape, F32, HBM), (small, F32, AUTO)],
-        [(inner_factor.shape, BF16), (inputs.shape, F32), (packed_more, F32), (inputs.shape, BF16)], 1 + rows // 2, flop, 6 * mib,
+        [(inner_factor.shape, BF16), (inputs.shape, F32), (packed_more, F32), (inputs.shape, BF16)], 1 + rows, flop, 6 * mib,
         (inner_factor, HBM), (back_got, AUTO), (inputs, AUTO), (cotangent, AUTO), (inv, AUTO), (gain, AUTO), (twiddle, AUTO),
     )
-    projection = lax.psum(part_proj, "chan")
+    projections = lax.all_gather(part_proj, "chan")
     input_grad, weight_grad = call(
         finish_kernel, s, "finish", [(inputs.shape, BF16, HBM), ((width, width), F32, HBM)],
         [(inputs.shape, F32), ((s.parts * width, LANES), F32), ((width, width), F32), (inputs.shape, BF16)],
-        rows + 2, flop // 100, 4 * mib,
-        (base, HBM), (whole.reshape(-1, LANES), HBM), (inputs, AUTO), (inv, AUTO), (projection, AUTO),
+        rows + rows // 2 + 2, flop // 100, 4 * mib,
+        (base, HBM), (whole.reshape(-1, LANES), HBM), (inputs, AUTO), (inv, AUTO), (projections, AUTO),
     )
     return (input_grad, weight_grad.reshape(1, width, width))
 

time: 163 us -> 162 us (level)
    all_gather x0 -> x2, blocking collectives: none -> 26.5 us  [the longest x1 15.8 us: on_device(): sums = lax.all_gather(part_sum, 'chan')]
    psum x2 -> x0, blocking collectives: 26.4 us -> none  [the longest x1 15.9 us: on_device(): sq_sum = lax.psum(part_sum, 'chan')]
where the time goes in v5:
time: 162 us; the launch traced here: 161 us
  blocking collectives  133 us (82%)
  Pallas kernels  17.3 us (11%)
  starting transfers between devices  7.64 us (5%)
  local copies, waits for them, and re-layouts  2 us (1%)
    all_to_all x2, blocking collectives, exchange(): lax.all_to_all(packed, 'seq', split_axis=0, concat_axis=0, tiled=True)  107 us
    pallas_call x5, Pallas kernels, call(): pl.pallas_call(functools.partial(kernel, s), out_shape=[(pltpu.HBM if pla...  17.3 us
    all_gather x1, blocking collectives, on_device(): sums = lax.all_gather(part_sum, 'chan')  15.8 us
    all_gather x1, blocking collectives, on_device(): projections = lax.all_gather(part_proj, 'chan')  10.7 us
    all_to_all x1, starting transfers between devices, on_device(): lax.all_to_all(jnp.broadcast_to(share, (seq,) + share.shape), 'seq', spli...  7.64 us
  transfers between devices with their start and end apart: 1, of which 0 were waited for; matrix products, arithmetic and copies ran while one was open for 0% of the time, Pallas kernels for 3%

profile of v5, /device:TPU:1, one launch (start us, length us, event | category | flops | bytes accessed | tf_op | source)
XLA Modules:
  0.0 161.3 jit_solution(15921292634253179503)
XLA Ops:
  0.6 0.0 copy-start
  0.6 1.2 copy-done
  1.9 0.7 squares.1
  2.5 15.8 %all-gather.2.sum_ref = f32[4,4,512]{2,1,0:T(4,128)S(1)} all-gather(f32[1,4,512]{2,1,0:T(4,128)S(1)} %bitcast.14), channel_id=2, replica_groups=mesh['seq'=128,'chan'=4] {'chan'}, dimensions={0}, use_global_device_ids=true | all-gather | bytes 40960 | tf_op jit(solution)/shard_map/all_gather | solution.py:257
  18.3 5.6 %inner.1 = (bf16[8192,128]{1,0:T(8,128)(2,1)S(1)}, f32[4,512]{1,0:T(4,128)S(1)}) custom-call(bf16[4,512,256]{2,1,0:T(8,128)(2,1)} %cot_ref.1, bf16[512,512]{1,0:T(8,128)(2,1)} %inner_hbm.3, bf16[4,512,256]{2,1,0:T(8,128)(2,1)} %x_ref.5, f32[1,256]{1,0:T(1,128)} %bitcast.16, f32[4,512]{1,0:T(4,128)} %tw_ref.1, f32[4,4,512]{2,1,0:T(4,128)S(1)} %all-gather.2.sum_ref), custom_call_target="tpu_custom_call" | custom-call | flops 536870912 | bytes 5242880 | tf_op jit(solution)/shard_map/inner/pallas_call | solution.py:224
  23.9 0.0 copy-start.5
  23.9 0.0 copy-start.6
  23.9 65.0 %all_to_all.15 = bf16[128,64,128]{2,1,0:T(8,128)(2,1)S(1)} all-to-all(bf16[128,64,128]{2,1,0:T(8,128)(2,1)S(1)} %bitcast.11), channel_id=1, replica_groups=mesh['seq'=128,'chan'=4] {'seq'}, dimensions={0} | all-to-all | bytes 4194304 | tf_op jit(solution)/shard_map/all_to_all | solution.py:241
  88.9 0.0 copy-done.5
  88.9 0.0 copy-done.6
  88.9 3.6 %middle.1 = bf16[5120,128]{1,0:T(8,128)(2,1)S(1)} custom-call(bf16[8192,128]{1,0:T(8,128)(2,1)S(1)} %bitcast.12, bf16[256,256]{1,0:T(8,128)(2,1)S(1)} %bitcast.18, bf16[512,512]{1,0:T(8,128)(2,1)S(1)} %copy-done.5), custom_call_target="tpu_custom_call" | custom-call | flops 1610612736 | bytes 4194304 | tf_op jit(solution)/shard_map/middle/pallas_call | solution.py:224
  92.5 0.0 copy-start.1
  92.5 0.0 copy-start.2
  92.5 0.0 copy-start.3
  92.5 0.0 copy-start.4
  92.5 41.8 %all_to_all.16 = bf16[128,40,128]{2,1,0:T(8,128)(2,1)S(1)} all-to-all(bf16[128,40,128]{2,1,0:T(8,128)(2,1)S(1)} %bitcast.13), channel_id=1, replica_groups=mesh['seq'=128,'chan'=4] {'seq'}, dimensions={0} | all-to-all | bytes 2621440 | tf_op jit(solution)/shard_map/all_to_all | solution.py:241
  134.3 0.1 convert_reduce_fusion
  134.5 0.7 broadcast_in_dim.3
  135.2 7.6 %all-to-all-start.2 = ((f32[128,4,128]{2,1,0:T(4,128)}), f32[128,4,128]{2,1,0:T(4,128)}, u32[]{:S(2)}, u32[]{:S(2)}) async-start(f32[128,4,128]{2,1,0:T(4,128)} %broadcast_in_dim.3), calls=%async_computation.2 | async-start | bytes 524288 | tf_op jit(solution)/shard_map/all_to_all | solution.py:274
  142.9 0.0 copy-done.1
  142.9 4.9 %back.1 = (f32[4,512,256]{2,1,0:T(8,128)}, f32[4,512]{1,0:T(4,128)S(1)}) custom-call(bf16[512,512]{1,0:T(8,128)(2,1)} %inner_hbm.3, bf16[5120,128]{1,0:T(8,128)(2,1)S(1)} %bitcast.10, bf16[4,512,256]{2,1,0:T(8,128)(2,1)S(1)} %copy-done.1, bf16[4,512,256]{2,1,0:T(8,128)(2,1)S(1)} %copy-done.2, f32[4,512]{1,0:T(4,128)S(1)} %get-tuple-element.9.inv_ref, ...), custom_call_target="tpu_custom_call" | custom-call | flops 536870912 | bytes 6291456 | tf_op jit(solution)/shard_map/back/pallas_call | solution.py:224
  147.8 10.7 %all-gather.3.proj_ref = f32[4,4,512]{2,1,0:T(4,128)S(1)} all-gather(f32[1,4,512]{2,1,0:T(4,128)S(1)} %bitcast.15), channel_id=3, replica_groups=mesh['seq'=128,'chan'=4] {'chan'}, dimensions={0}, use_global_device_ids=true | all-gather | bytes 40960 | tf_op jit(solution)/shard_map/all_gather | solution.py:282
  158.6 0.0 all-to-all-done.2
  158.6 2.6 %finish.1 = (bf16[4,512,256]{2,1,0:T(8,128)(2,1)}, f32[256,256]{1,0:T(8,128)}) custom-call(f32[4,512,256]{2,1,0:T(8,128)} %get-tuple-element.10.sum_hbm, f32[512,128]{1,0:T(8,128)} %bitcast.7.whole_hbm, bf16[4,512,256]{2,1,0:T(8,128)(2,1)S(1)} %copy-done.1, f32[4,512]{1,0:T(4,128)S(1)} %get-tuple-element.9.inv_ref, f32[4,4,512]{2,1,0:T(4,128)S(1)} %all-gather.3.proj_ref), custom_call_target="tpu_custom_call" | custom-call | flops 5368709 | bytes 4194304 | tf_op jit(solution)/shard_map/finish/pallas_call | solution.py:224
  (4 shorter events, 0.0 us)
Async XLA Ops:
  0.6 1.2 copy-start
  23.9 65.0 %copy-start.5 = (bf16[512,512]{1,0:T(8,128)(2,1)S(1)}, bf16[512,512]{1,0:T(8,128)(2,1)}, u32[]{:S(2)}) copy-start(bf16[512,512]{1,0:T(8,128)(2,1)} %outer_ref.1) | copy-start | bytes 1572868
  23.9 65.0 %copy-start.6 = (bf16[1,256,256]{2,1,0:T(8,128)(2,1)S(1)}, bf16[1,256,256]{2,1,0:T(8,128)(2,1)}, u32[]{:S(2)}) copy-start(bf16[1,256,256]{2,1,0:T(8,128)(2,1)} %param.12) | copy-start | bytes 393220
  92.5 50.4 %copy-start.1 = (bf16[4,512,256]{2,1,0:T(8,128)(2,1)S(1)}, bf16[4,512,256]{2,1,0:T(8,128)(2,1)}, u32[]{:S(2)}) copy-start(bf16[4,512,256]{2,1,0:T(8,128)(2,1)} %x_ref.5) | copy-start | bytes 3145732
  92.5 50.4 %copy-start.2 = (bf16[4,512,256]{2,1,0:T(8,128)(2,1)S(1)}, bf16[4,512,256]{2,1,0:T(8,128)(2,1)}, u32[]{:S(2)}) copy-start(bf16[4,512,256]{2,1,0:T(8,128)(2,1)} %cot_ref.1) | copy-start | bytes 3145732
  92.5 50.4 %copy-start.3 = (f32[4,512]{1,0:T(4,128)S(1)}, f32[4,512]{1,0:T(4,128)}, u32[]{:S(2)}) copy-start(f32[4,512]{1,0:T(4,128)} %tw_ref.1) | copy-start | bytes 24580
  92.5 50.4 %copy-start.4 = (f32[256]{0:T(256)S(1)}, f32[256]{0:T(256)}, u32[]{:S(2)}) copy-start(f32[256]{0:T(256)} %param.8) | copy-start | bytes 3076
  135.2 23.4 %all-to-all-start.2 = ((f32[128,4,128]{2,1,0:T(4,128)}), f32[128,4,128]{2,1,0:T(4,128)}, u32[]{:S(2)}, u32[]{:S(2)}) async-start(f32[128,4,128]{2,1,0:T(4,128)} %broadcast_in_dim.3), calls=%async_computation.2 | async-start | bytes 524288 | tf_op jit(solution)/shard_map/all_to_all | solution.py:274

commit v6 on v5

--- a/solution.py
+++ b/solution.py
@@ -37,7 +37,6 @@
         self.cols = n2 // seq
         self.parts = width // LANES
         self.block = self.cols * self.parts * rows
-        self.extra = 2 * (width // seq) * self.parts
 
     def pieces(self):
         for jh in range(self.cols):
@@ -123,7 +122,13 @@
     return jnp.where(a == lax.broadcasted_iota(jnp.int32, (n, n), 1), 1.0, 0.0).astype(BF16)
 
 
-def middle_kernel(s, got_ref, weight_ref, outer_ref, send_ref, part_ref, out_ref):
+def put(out_ref, q, v):
+    v = v.reshape(-1, 8, LANES)
+    out_ref[:, 0, q] = v[:, :4]
+    out_ref[:, 1, q] = v[:, 4:]
+
+
+def middle_kernel(s, got_ref, weight_ref, outer_ref, send_ref, part_ref, out_ref, piece_ref):
     n1 = s.seq * s.rows
     outer_t = dot(unit(n1), outer_ref[...], 1, 1).astype(BF16)
     tiles = s.block // 8
@@ -150,21 +155,16 @@
             term = product[:, part * LANES : (part + 1) * LANES]
             part_ref[here, :] = term if jh == 0 else part_ref[here, :] + term
         back = dot(outer_t, grad, 1, 0)
-        even, odd = swap_halves(
-            back[:, :LANES].reshape(n1 // 8, 8, LANES), back[:, LANES:].reshape(n1 // 8, 8, LANES)
-        )
-        out_ref[:, 0, jh] = even
-        out_ref[:, 1, jh] = odd
+        for part in range(s.parts):
+            put(out_ref, jh * s.parts + part, back[:, part * LANES : (part + 1) * LANES])
     step = s.width // s.seq
-    flat = out_ref.reshape(s.seq * (s.block + s.extra), LANES)
     for i in range(step):
         for part in range(s.parts):
-            at = s.block + i * s.parts + part
-            v = part_ref[pl.ds(part * s.width + i, s.seq, step), :]
-            hi = v.astype(BF16).astype(F32)
-            flat[pl.ds(at, s.seq, s.block + s.extra), :] = hi
-            flat[pl.ds(at + s.extra // 2, s.seq, s.block + s.extra), :] = v - hi
-    send_ref[...] = flat[...].astype(BF16)
+            piece_ref[pl.ds(i * s.parts + part, s.seq, step * s.parts), :] = part_ref[
+                pl.ds(part * s.width + i, s.seq, step), :
+            ]
+    put(out_ref, s.cols * s.parts, piece_ref[...])
+    send_ref[...] = out_ref[...].astype(BF16)
 
 
 def back_kernel(
@@ -173,15 +173,17 @@
 ):
     copies = Copies(sems)
     load = copies.start(inner_hbm, inner_ref)
-    wide_ref[...] = got_ref[...].astype(F32)
-    full = s.block + s.extra
+    tiles = wide_ref.reshape(s.seq, s.block // 8, 8, LANES)
+    for p in range(s.block // 8):
+        both = [got_ref[:, :, q].astype(F32) for q in (2 * p, 2 * p + 1)]
+        tiles[:, p] = jnp.concatenate(both, axis=2).reshape(s.seq, 8, LANES)
     inv_cols = column_form(inv_ref[...])
     tw_cols = column_form(tw_ref[...])
     for r in range(s.rows):
         for jh, part, q in s.pieces():
             here = slice(jh * s.seq, (jh + 1) * s.seq)
             col_ref[r, here, part * LANES : (part + 1) * LANES] = (
-                wide_ref[pl.ds(q + r, s.seq, full), :] * tw_cols[here, r : r + 1]
+                wide_ref[pl.ds(q + r, s.seq, s.block), :] * tw_cols[here, r : r + 1]
             ).astype(BF16)
     load.wait()
     inner_t = dot(unit(s.n2), inner_ref[...], 1, 1).astype(BF16)
@@ -245,7 +247,8 @@
     rows, n2, width = inputs.shape
     s = Sizes(seq, rows, n2, width)
     packed_two = (2 * seq * s.block, LANES)
-    packed_more = (seq * (s.block + s.extra), LANES)
+    groups = s.cols * s.parts + 1
+    sent = (seq // 2, 2, groups, rows, LANES)
     mib = rows * n2 * width * 2
     flop = 2 * rows * n2 * n2 * width
     gain = norm_gain.reshape(1, width)
@@ -263,20 +266,20 @@
     )
     got = exchange(send, seq)
     (back_send,) = call(
-        middle_kernel, s, "middle", [(packed_more, BF16, AUTO)],
-        [((s.parts * width, LANES), F32), ((seq // 2, 2, (s.block + s.extra) // 8, 8, LANES), F32)], 0, 3 * flop, 4 * mib,
+        middle_kernel, s, "middle", [(sent, BF16, AUTO)],
+        [((s.parts * width, LANES), F32), (sent, F32), ((rows * seq, LANES), F32)], 0, 3 * flop, 4 * mib,
         (got, AUTO), (channel_weight[0], AUTO), (outer_factor, AUTO),
     )
-    back_got = exchange(back_send, seq)
-    pairs = back_got.reshape(seq, s.block + s.extra, LANES)[:, s.block :].astype(F32)
-    pairs = jnp.sum(pairs, axis=0)
-    share = pairs[: s.extra // 2] + pairs[s.extra // 2 :]
+    back_got = lax.all_to_all(
+        back_send.reshape(seq * groups, rows, LANES), "seq", split_axis=0, concat_axis=0, tiled=True
+    ).reshape(sent)
+    share = jnp.sum(back_got[:, :, -1].astype(F32), axis=(0, 1))
     whole = lax.all_to_all(
         jnp.broadcast_to(share, (seq,) + share.shape), "seq", split_axis=0, concat_axis=0, tiled=True
     )
     base, part_proj = call(
         back_kernel, s, "back", [(inputs.shape, F32, HBM), (small, F32, AUTO)],
-        [(inner_factor.shape, BF16), (inputs.shape, F32), (packed_more, F32), (inputs.shape, BF16)], 1 + rows, flop, 6 * mib,
+        [(inner_factor.shape, BF16), (inputs.shape, F32), ((seq * s.block, LANES), F32), (inputs.shape, BF16)], 1 + rows, flop, 6 * mib,
         (inner_factor, HBM), (back_got, AUTO), (inputs, AUTO), (cotangent, AUTO), (inv, AUTO), (gain, AUTO), (twiddle, AUTO),
     )
     projections = lax.all_gather(part_proj, "chan")

time: 162 us -> 160 us (0.988)
  blocking collectives: 133 us -> 131 us
    all_to_all x2 -> x1, blocking collectives: 107 us -> 65 us  [exchange(): lax.all_to_all(packed, 'seq', split_axis=0, concat_axis=0, tiled=True)]
    all_to_all x0 -> x1, blocking collectives: none -> 39 us  [on_device(): lax.all_to_all(back_send.reshape(seq * groups, rows, LANES), 'seq', split...]
where the time goes in v6:
time: 160 us; the launch traced here: 159 us
  blocking collectives  131 us (82%)
  Pallas kernels  18 us (11%)
  starting transfers between devices  7.74 us (5%)
  local copies, waits for them, and re-layouts  2 us (1%)
    all_to_all x1, blocking collectives, exchange(): lax.all_to_all(packed, 'seq', split_axis=0, concat_axis=0, tiled=True)  65 us
    all_to_all x1, blocking collectives, on_device(): lax.all_to_all(back_send.reshape(seq * groups, rows, LANES), 'seq', split...  39 us
    pallas_call x5, Pallas kernels, call(): pl.pallas_call(functools.partial(kernel, s), out_shape=[(pltpu.HBM if pla...  18 us
    all_gather x1, blocking collectives, on_device(): sums = lax.all_gather(part_sum, 'chan')  15.8 us
    all_gather x1, blocking collectives, on_device(): projections = lax.all_gather(part_proj, 'chan')  10.8 us
    all_to_all x1, starting transfers between devices, on_device(): lax.all_to_all(jnp.broadcast_to(share, (seq,) + share.shape), 'seq', spli...  7.74 us
  transfers between devices with their start and end apart: 1, of which 0 were waited for; matrix products, arithmetic and copies ran while one was open for 0% of the time, Pallas kernels for 3%

profile of v6, /device:TPU:1, one launch (start us, length us, event | category | flops | bytes accessed | tf_op | source)
XLA Modules:
  0.0 159.4 jit_solution(9652201955887963468)
XLA Ops:
  0.6 0.0 copy-start
  0.6 1.2 copy-done
  1.9 0.7 squares.1
  2.5 15.8 %all-gather.2.sum_ref = f32[4,4,512]{2,1,0:T(4,128)S(1)} all-gather(f32[1,4,512]{2,1,0:T(4,128)S(1)} %bitcast.15), channel_id=2, replica_groups=mesh['seq'=128,'chan'=4] {'chan'}, dimensions={0}, use_global_device_ids=true | all-gather | bytes 40960 | tf_op jit(solution)/shard_map/all_gather | solution.py:260
  18.3 5.6 %inner.1 = (bf16[8192,128]{1,0:T(8,128)(2,1)S(1)}, f32[4,512]{1,0:T(4,128)S(1)}) custom-call(bf16[4,512,256]{2,1,0:T(8,128)(2,1)} %cot_ref.1, bf16[512,512]{1,0:T(8,128)(2,1)} %inner_hbm.3, bf16[4,512,256]{2,1,0:T(8,128)(2,1)} %x_ref.5, f32[1,256]{1,0:T(1,128)} %bitcast.17, f32[4,512]{1,0:T(4,128)} %tw_ref.1, f32[4,4,512]{2,1,0:T(4,128)S(1)} %all-gather.2.sum_ref), custom_call_target="tpu_custom_call" | custom-call | flops 536870912 | bytes 5242880 | tf_op jit(solution)/shard_map/inner/pallas_call | solution.py:226
  23.9 0.0 copy-start.5
  23.9 0.0 copy-start.6
  23.9 65.0 %all_to_all.15 = bf16[128,64,128]{2,1,0:T(8,128)(2,1)S(1)} all-to-all(bf16[128,64,128]{2,1,0:T(8,128)(2,1)S(1)} %bitcast.12), channel_id=1, replica_groups=mesh['seq'=128,'chan'=4] {'seq'}, dimensions={0} | all-to-all | bytes 4194304 | tf_op jit(solution)/shard_map/all_to_all | solution.py:243
  88.9 0.0 copy-done.5
  88.9 0.0 copy-done.6
  88.9 3.9 %middle.1 = bf16[64,2,9,4,128]{4,3,2,1,0:T(4,128)(2,1)S(1)} custom-call(bf16[8192,128]{1,0:T(8,128)(2,1)S(1)} %bitcast.13, bf16[256,256]{1,0:T(8,128)(2,1)S(1)} %bitcast.19, bf16[512,512]{1,0:T(8,128)(2,1)S(1)} %copy-done.5), custom_call_target="tpu_custom_call" | custom-call | flops 1610612736 | bytes 4194304 | tf_op jit(solution)/shard_map/middle/pallas_call | solution.py:226
  92.8 0.0 copy-start.1
  92.9 0.0 copy-start.2
  92.9 0.0 copy-start.3
  92.9 0.0 copy-start.4
  92.9 39.0 %all_to_all.16 = bf16[1152,4,128]{2,1,0:T(4,128)(2,1)S(1)} all-to-all(bf16[1152,4,128]{2,1,0:T(4,128)(2,1)S(1)} %bitcast.14), channel_id=1, replica_groups=mesh['seq'=128,'chan'=4] {'seq'}, dimensions={0} | all-to-all | bytes 2359296 | tf_op jit(solution)/shard_map/all_to_all | solution.py:273
  131.9 0.1 convert_reduce_fusion
  132.1 0.7 broadcast_in_dim.3
  132.8 7.7 %all-to-all-start.2 = ((f32[128,4,128]{2,1,0:T(4,128)}), f32[128,4,128]{2,1,0:T(4,128)}, u32[]{:S(2)}, u32[]{:S(2)}) async-start(f32[128,4,128]{2,1,0:T(4,128)} %broadcast_in_dim.3), calls=%async_computation.2 | async-start | bytes 524288 | tf_op jit(solution)/shard_map/all_to_all | solution.py:277
  140.6 0.0 copy-done.1
  140.6 5.2 %back.1 = (f32[4,512,256]{2,1,0:T(8,128)}, f32[4,512]{1,0:T(4,128)S(1)}) custom-call(bf16[512,512]{1,0:T(8,128)(2,1)} %inner_hbm.3, bf16[64,2,9,4,128]{4,3,2,1,0:T(4,128)(2,1)S(1)} %bitcast.11, bf16[4,512,256]{2,1,0:T(8,128)(2,1)S(1)} %copy-done.1, bf16[4,512,256]{2,1,0:T(8,128)(2,1)S(1)} %copy-done.2, f32[4,512]{1,0:T(4,128)S(1)} %get-tuple-element.9.inv_ref, ...), custom_call_target="tpu_custom_call" | custom-call | flops 536870912 | bytes 6291456 | tf_op jit(solution)/shard_map/back/pallas_call | solution.py:226
  145.8 10.8 %all-gather.3.proj_ref = f32[4,4,512]{2,1,0:T(4,128)S(1)} all-gather(f32[1,4,512]{2,1,0:T(4,128)S(1)} %bitcast.16), channel_id=3, replica_groups=mesh['seq'=128,'chan'=4] {'chan'}, dimensions={0}, use_global_device_ids=true | all-gather | bytes 40960 | tf_op jit(solution)/shard_map/all_gather | solution.py:285
  156.6 0.0 all-to-all-done.2
  156.6 2.6 %finish.1 = (bf16[4,512,256]{2,1,0:T(8,128)(2,1)}, f32[256,256]{1,0:T(8,128)}) custom-call(f32[4,512,256]{2,1,0:T(8,128)} %get-tuple-element.10.sum_hbm, f32[512,128]{1,0:T(8,128)} %bitcast.7.whole_hbm, bf16[4,512,256]{2,1,0:T(8,128)(2,1)S(1)} %copy-done.1, f32[4,512]{1,0:T(4,128)S(1)} %get-tuple-element.9.inv_ref, f32[4,4,512]{2,1,0:T(4,128)S(1)} %all-gather.3.proj_ref), custom_call_target="tpu_custom_call" | custom-call | flops 5368709 | bytes 4194304 | tf_op jit(solution)/shard_map/finish/pallas_call | solution.py:226
  (3 shorter events, 0.0 us)
Async XLA Ops:
  0.6 1.2 copy-start
  23.9 65.0 %copy-start.5 = (bf16[512,512]{1,0:T(8,128)(2,1)S(1)}, bf16[512,512]{1,0:T(8,128)(2,1)}, u32[]{:S(2)}) copy-start(bf16[512,512]{1,0:T(8,128)(2,1)} %outer_ref.1) | copy-start | bytes 1572868
  23.9 65.0 %copy-start.6 = (bf16[1,256,256]{2,1,0:T(8,128)(2,1)S(1)}, bf16[1,256,256]{2,1,0:T(8,128)(2,1)}, u32[]{:S(2)}) copy-start(bf16[1,256,256]{2,1,0:T(8,128)(2,1)} %param.12) | copy-start | bytes 393220
  92.8 47.7 %copy-start.1 = (bf16[4,512,256]{2,1,0:T(8,128)(2,1)S(1)}, bf16[4,512,256]{2,1,0:T(8,128)(2,1)}, u32[]{:S(2)}) copy-start(bf16[4,512,256]{2,1,0:T(8,128)(2,1)} %x_ref.5) | copy-start | bytes 3145732
  92.9 47.7 %copy-start.2 = (bf16[4,512,256]{2,1,0:T(8,128)(2,1)S(1)}, bf16[4,512,256]{2,1,0:T(8,128)(2,1)}, u32[]{:S(2)}) copy-start(bf16[4,512,256]{2,1,0:T(8,128)(2,1)} %cot_ref.1) | copy-start | bytes 3145732
  92.9 47.7 %copy-start.3 = (f32[4,512]{1,0:T(4,128)S(1)}, f32[4,512]{1,0:T(4,128)}, u32[]{:S(2)}) copy-start(f32[4,512]{1,0:T(4,128)} %tw_ref.1) | copy-start | bytes 24580
  92.9 47.7 %copy-start.4 = (f32[256]{0:T(256)S(1)}, f32[256]{0:T(256)}, u32[]{:S(2)}) copy-start(f32[256]{0:T(256)} %param.8) | copy-start | bytes 3076
  132.8 23.8 %all-to-all-start.2 = ((f32[128,4,128]{2,1,0:T(4,128)}), f32[128,4,128]{2,1,0:T(4,128)}, u32[]{:S(2)}, u32[]{:S(2)}) async-start(f32[128,4,128]{2,1,0:T(4,128)} %broadcast_in_dim.3), calls=%async_computation.2 | async-start | bytes 524288 | tf_op jit(solution)/shard_map/all_to_all | solution.py:277

commit v7 on v6

--- a/solution.py
+++ b/solution.py
@@ -81,8 +81,7 @@
     cot_ref, inner_ref, x_ref, gain_ref, tw_ref, wide_ref, sems,
 ):
     copies = Copies(sems)
-    pairs = [slice(r, r + 2) for r in range(0, s.rows, 2)]
-    cot_loads = [copies.start(cot_hbm.at[pair], cot_ref.at[pair]) for pair in pairs]
+    cot_loads = [copies.start(cot_hbm.at[r], cot_ref.at[r]) for r in range(s.rows)]
     tw_load = copies.start(tw_hbm, tw_ref)
     gain_load = copies.start(gain_hbm, gain_ref)
     inner_load = copies.start(inner_hbm, inner_ref)
@@ -91,8 +90,7 @@
     inv_ref[...] = inv
     inv_cols = column_form(inv)
     for r in range(s.rows):
-        if r % 2 == 0:
-            cot_loads[r // 2].wait()
+        cot_loads[r].wait()
         for jh, part, q in s.pieces():
             wide_ref[pl.ds(s.block + q + r, s.seq, 2 * s.block), :] = cot_ref[
                 r, jh * s.seq : (jh + 1) * s.seq, part * LANES : (part + 1) * LANES
@@ -124,11 +122,11 @@
 
 def put(out_ref, q, v):
     v = v.reshape(-1, 8, LANES)
-    out_ref[:, 0, q] = v[:, :4]
-    out_ref[:, 1, q] = v[:, 4:]
-
-
-def middle_kernel(s, got_ref, weight_ref, outer_ref, send_ref, part_ref, out_ref, piece_ref):
+    out_ref[:, 0, q] = v[:, :4].astype(BF16)
+    out_ref[:, 1, q] = v[:, 4:].astype(BF16)
+
+
+def middle_kernel(s, got_ref, weight_ref, outer_ref, send_ref, part_ref, piece_ref):
     n1 = s.seq * s.rows
     outer_t = dot(unit(n1), outer_ref[...], 1, 1).astype(BF16)
     tiles = s.block // 8
@@ -156,15 +154,14 @@
             part_ref[here, :] = term if jh == 0 else part_ref[here, :] + term
         back = dot(outer_t, grad, 1, 0)
         for part in range(s.parts):
-            put(out_ref, jh * s.parts + part, back[:, part * LANES : (part + 1) * LANES])
+            put(send_ref, jh * s.parts + part, back[:, part * LANES : (part + 1) * LANES])
     step = s.width // s.seq
     for i in range(step):
         for part in range(s.parts):
             piece_ref[pl.ds(i * s.parts + part, s.seq, step * s.parts), :] = part_ref[
                 pl.ds(part * s.width + i, s.seq, step), :
             ]
-    put(out_ref, s.cols * s.parts, piece_ref[...])
-    send_ref[...] = out_ref[...].astype(BF16)
+    put(send_ref, s.cols * s.parts, piece_ref[...])
 
 
 def back_kernel(
@@ -201,20 +198,18 @@
     s, sum_hbm, whole_hbm, x_ref, inv_ref, proj_ref, out_hbm, weight_hbm, sum_ref, whole_ref, weight_ref, out_ref, sems
 ):
     copies = Copies(sems)
+    whole_load = copies.start(whole_hbm, whole_ref)
     sum_loads = [copies.start(sum_hbm.at[r], sum_ref.at[r]) for r in range(s.rows)]
-    whole_load = copies.start(whole_hbm, whole_ref)
     inv = inv_ref[...]
     factor = column_form(inv * inv * inv * total(proj_ref) / D)
-    stores = []
-    for r in range(s.rows):
-        sum_loads[r].wait()
-        out_ref[r] = (sum_ref[r] - x_ref[r].astype(F32) * factor[:, r : r + 1]).astype(BF16)
-        if r % 2 == 1:
-            stores.append(copies.start(out_ref.at[r - 1 : r + 1], out_hbm.at[r - 1 : r + 1]))
     whole_load.wait()
     for part in range(s.parts):
         weight_ref[:, part * LANES : (part + 1) * LANES] = whole_ref[pl.ds(part, s.width, s.parts), :]
-    stores.append(copies.start(weight_ref, weight_hbm))
+    stores = [copies.start(weight_ref, weight_hbm)]
+    for r in range(s.rows):
+        sum_loads[r].wait()
+        out_ref[r] = (sum_ref[r] - x_ref[r].astype(F32) * factor[:, r : r + 1]).astype(BF16)
+        stores.append(copies.start(out_ref.at[r], out_hbm.at[r]))
     wait(stores)
 
 
@@ -261,13 +256,13 @@
     send, inv = call(
         inner_kernel, s, "inner", [(packed_two, BF16, AUTO), (small, F32, AUTO)],
         [(inputs.shape, BF16), (inner_factor.shape, BF16), (inputs.shape, BF16), (gain.shape, F32), (small, F32), (packed_two, F32)],
-        4 + rows // 2, flop, 5 * mib,
+        4 + rows, flop, 5 * mib,
         (cotangent, HBM), (inner_factor, HBM), (inputs, HBM), (gain, HBM), (twiddle, HBM), (sums, AUTO),
     )
     got = exchange(send, seq)
     (back_send,) = call(
         middle_kernel, s, "middle", [(sent, BF16, AUTO)],
-        [((s.parts * width, LANES), F32), (sent, F32), ((rows * seq, LANES), F32)], 0, 3 * flop, 4 * mib,
+        [((s.parts * width, LANES), F32), ((rows * seq, LANES), F32)], 0, 3 * flop, 4 * mib,
         (got, AUTO), (channel_weight[0], AUTO), (outer_factor, AUTO),
     )
     back_got = lax.all_to_all(
@@ -286,7 +281,7 @@
     input_grad, weight_grad = call(
         finish_kernel, s, "finish", [(inputs.shape, BF16, HBM), ((width, width), F32, HBM)],
         [(inputs.shape, F32), ((s.parts * width, LANES), F32), ((width, width), F32), (inputs.shape, BF16)],
-        rows + rows // 2 + 2, flop // 100, 4 * mib,
+        2 * rows + 2, flop // 100, 4 * mib,
         (base, HBM), (whole.reshape(-1, LANES), HBM), (inputs, AUTO), (inv, AUTO), (projections, AUTO),
     )
     return (input_grad, weight_grad.reshape(1, width, width))

time: 160 us -> 159 us (level)
  no operation moved by 1% of the time
where the time goes in v7:
time: 159 us
  blocking collectives  131 us (82%)
  Pallas kernels  17.5 us (11%)
  starting transfers between devices  7.74 us (5%)
  local copies, waits for them, and re-layouts  2 us (1%)
    all_to_all x1, blocking collectives, exchange(): lax.all_to_all(packed, 'seq', split_axis=0, concat_axis=0, tiled=True)  65 us
    all_to_all x1, blocking collectives, on_device(): lax.all_to_all(back_send.reshape(seq * groups, rows, LANES), 'seq', split...  39 us
    pallas_call x5, Pallas kernels, call(): pl.pallas_call(functools.partial(kernel, s), out_shape=[(pltpu.HBM if pla...  17.5 us
    all_gather x1, blocking collectives, on_device(): sums = lax.all_gather(part_sum, 'chan')  15.8 us
    all_gather x1, blocking collectives, on_device(): projections = lax.all_gather(part_proj, 'chan')  10.8 us
    all_to_all x1, starting transfers between devices, on_device(): lax.all_to_all(jnp.broadcast_to(share, (seq,) + share.shape), 'seq', spli...  7.74 us
  transfers between devices with their start and end apart: 1, of which 0 were waited for; matrix products, arithmetic and copies ran while one was open for 0% of the time, Pallas kernels for 3%

profile of v7, /device:TPU:1, one launch (start us, length us, event | category | flops | bytes accessed | tf_op | source)
XLA Modules:
  0.0 158.8 jit_solution(14975877651882178872)
XLA Ops:
  0.6 0.0 copy-start
  0.6 1.2 copy-done
  1.9 0.7 squares.1
  2.5 15.8 %all-gather.2.sum_ref = f32[4,4,512]{2,1,0:T(4,128)S(1)} all-gather(f32[1,4,512]{2,1,0:T(4,128)S(1)} %bitcast.15), channel_id=2, replica_groups=mesh['seq'=128,'chan'=4] {'chan'}, dimensions={0}, use_global_device_ids=true | all-gather | bytes 40960 | tf_op jit(solution)/shard_map/all_gather | solution.py:255
  18.3 5.5 %inner.1 = (bf16[8192,128]{1,0:T(8,128)(2,1)S(1)}, f32[4,512]{1,0:T(4,128)S(1)}) custom-call(bf16[4,512,256]{2,1,0:T(8,128)(2,1)} %cot_ref.1, bf16[512,512]{1,0:T(8,128)(2,1)} %inner_hbm.3, bf16[4,512,256]{2,1,0:T(8,128)(2,1)} %x_ref.5, f32[1,256]{1,0:T(1,128)} %bitcast.17, f32[4,512]{1,0:T(4,128)} %tw_ref.1, f32[4,4,512]{2,1,0:T(4,128)S(1)} %all-gather.2.sum_ref), custom_call_target="tpu_custom_call" | custom-call | flops 536870912 | bytes 5242880 | tf_op jit(solution)/shard_map/inner/pallas_call | solution.py:221
  23.8 0.0 copy-start.5
  23.8 0.0 copy-start.6
  23.8 65.0 %all_to_all.15 = bf16[128,64,128]{2,1,0:T(8,128)(2,1)S(1)} all-to-all(bf16[128,64,128]{2,1,0:T(8,128)(2,1)S(1)} %bitcast.12), channel_id=1, replica_groups=mesh['seq'=128,'chan'=4] {'seq'}, dimensions={0} | all-to-all | bytes 4194304 | tf_op jit(solution)/shard_map/all_to_all | solution.py:238
  88.8 0.0 copy-done.5
  88.8 0.0 copy-done.6
  88.8 3.5 %middle.1 = bf16[64,2,9,4,128]{4,3,2,1,0:T(4,128)(2,1)S(1)} custom-call(bf16[8192,128]{1,0:T(8,128)(2,1)S(1)} %bitcast.13, bf16[256,256]{1,0:T(8,128)(2,1)S(1)} %bitcast.19, bf16[512,512]{1,0:T(8,128)(2,1)S(1)} %copy-done.5), custom_call_target="tpu_custom_call" | custom-call | flops 1610612736 | bytes 4194304 | tf_op jit(solution)/shard_map/middle/pallas_call | solution.py:221
  92.3 0.0 copy-start.1
  92.4 0.0 copy-start.2
  92.4 0.0 copy-start.3
  92.4 0.0 copy-start.4
  92.4 39.0 %all_to_all.16 = bf16[1152,4,128]{2,1,0:T(4,128)(2,1)S(1)} all-to-all(bf16[1152,4,128]{2,1,0:T(4,128)(2,1)S(1)} %bitcast.14), channel_id=1, replica_groups=mesh['seq'=128,'chan'=4] {'seq'}, dimensions={0} | all-to-all | bytes 2359296 | tf_op jit(solution)/shard_map/all_to_all | solution.py:268
  131.4 0.1 convert_reduce_fusion
  131.6 0.7 broadcast_in_dim.3
  132.3 7.7 %all-to-all-start.2 = ((f32[128,4,128]{2,1,0:T(4,128)}), f32[128,4,128]{2,1,0:T(4,128)}, u32[]{:S(2)}, u32[]{:S(2)}) async-start(f32[128,4,128]{2,1,0:T(4,128)} %broadcast_in_dim.3), calls=%async_computation.2 | async-start | bytes 524288 | tf_op jit(solution)/shard_map/all_to_all | solution.py:272
  140.1 0.0 copy-done.1
  140.1 5.2 %back.1 = (f32[4,512,256]{2,1,0:T(8,128)}, f32[4,512]{1,0:T(4,128)S(1)}) custom-call(bf16[512,512]{1,0:T(8,128)(2,1)} %inner_hbm.3, bf16[64,2,9,4,128]{4,3,2,1,0:T(4,128)(2,1)S(1)} %bitcast.11, bf16[4,512,256]{2,1,0:T(8,128)(2,1)S(1)} %copy-done.1, bf16[4,512,256]{2,1,0:T(8,128)(2,1)S(1)} %copy-done.2, f32[4,512]{1,0:T(4,128)S(1)} %get-tuple-element.9.inv_ref, ...), custom_call_target="tpu_custom_call" | custom-call | flops 536870912 | bytes 6291456 | tf_op jit(solution)/shard_map/back/pallas_call | solution.py:221
  145.3 10.8 %all-gather.3.proj_ref = f32[4,4,512]{2,1,0:T(4,128)S(1)} all-gather(f32[1,4,512]{2,1,0:T(4,128)S(1)} %bitcast.16), channel_id=3, replica_groups=mesh['seq'=128,'chan'=4] {'chan'}, dimensions={0}, use_global_device_ids=true | all-gather | bytes 40960 | tf_op jit(solution)/shard_map/all_gather | solution.py:280
  156.1 0.0 all-to-all-done.2
  156.1 2.5 %finish.1 = (bf16[4,512,256]{2,1,0:T(8,128)(2,1)}, f32[256,256]{1,0:T(8,128)}) custom-call(f32[4,512,256]{2,1,0:T(8,128)} %get-tuple-element.10.sum_hbm, f32[512,128]{1,0:T(8,128)} %bitcast.7.whole_hbm, bf16[4,512,256]{2,1,0:T(8,128)(2,1)S(1)} %copy-done.1, f32[4,512]{1,0:T(4,128)S(1)} %get-tuple-element.9.inv_ref, f32[4,4,512]{2,1,0:T(4,128)S(1)} %all-gather.3.proj_ref), custom_call_target="tpu_custom_call" | custom-call | flops 5368709 | bytes 4194304 | tf_op jit(solution)/shard_map/finish/pallas_call | solution.py:221
  (3 shorter events, 0.0 us)
Async XLA Ops:
  0.6 1.2 copy-start
  23.8 65.0 %copy-start.5 = (bf16[512,512]{1,0:T(8,128)(2,1)S(1)}, bf16[512,512]{1,0:T(8,128)(2,1)}, u32[]{:S(2)}) copy-start(bf16[512,512]{1,0:T(8,128)(2,1)} %outer_ref.1) | copy-start | bytes 1572868
  23.8 65.0 %copy-start.6 = (bf16[1,256,256]{2,1,0:T(8,128)(2,1)S(1)}, bf16[1,256,256]{2,1,0:T(8,128)(2,1)}, u32[]{:S(2)}) copy-start(bf16[1,256,256]{2,1,0:T(8,128)(2,1)} %param.12) | copy-start | bytes 393220
  92.3 47.7 %copy-start.1 = (bf16[4,512,256]{2,1,0:T(8,128)(2,1)S(1)}, bf16[4,512,256]{2,1,0:T(8,128)(2,1)}, u32[]{:S(2)}) copy-start(bf16[4,512,256]{2,1,0:T(8,128)(2,1)} %x_ref.5) | copy-start | bytes 3145732
  92.4 47.7 %copy-start.2 = (bf16[4,512,256]{2,1,0:T(8,128)(2,1)S(1)}, bf16[4,512,256]{2,1,0:T(8,128)(2,1)}, u32[]{:S(2)}) copy-start(bf16[4,512,256]{2,1,0:T(8,128)(2,1)} %cot_ref.1) | copy-start | bytes 3145732
  92.4 47.7 %copy-start.3 = (f32[4,512]{1,0:T(4,128)S(1)}, f32[4,512]{1,0:T(4,128)}, u32[]{:S(2)}) copy-start(f32[4,512]{1,0:T(4,128)} %tw_ref.1) | copy-start | bytes 24580
  92.4 47.7 %copy-start.4 = (f32[256]{0:T(256)S(1)}, f32[256]{0:T(256)}, u32[]{:S(2)}) copy-start(f32[256]{0:T(256)} %param.8) | copy-start | bytes 3076
  132.3 23.8 %all-to-all-start.2 = ((f32[128,4,128]{2,1,0:T(4,128)}), f32[128,4,128]{2,1,0:T(4,128)}, u32[]{:S(2)}, u32[]{:S(2)}) async-start(f32[128,4,128]{2,1,0:T(4,128)} %broadcast_in_dim.3), calls=%async_computation.2 | async-start | bytes 524288 | tf_op jit(solution)/shard_map/all_to_all | solution.py:272

commit v8 on v7

--- a/solution.py
+++ b/solution.py
@@ -115,11 +115,6 @@
     )
 
 
-def unit(n):
-    a = lax.broadcasted_iota(jnp.int32, (n, n), 0)
-    return jnp.where(a == lax.broadcasted_iota(jnp.int32, (n, n), 1), 1.0, 0.0).astype(BF16)
-
-
 def put(out_ref, q, v):
     v = v.reshape(-1, 8, LANES)
     out_ref[:, 0, q] = v[:, :4].astype(BF16)
@@ -128,7 +123,7 @@
 
 def middle_kernel(s, got_ref, weight_ref, outer_ref, send_ref, part_ref, piece_ref):
     n1 = s.seq * s.rows
-    outer_t = dot(unit(n1), outer_ref[...], 1, 1).astype(BF16)
+    outer_t = outer_ref[...].T
     tiles = s.block // 8
     got = got_ref[...].reshape(s.seq // 2, 2, 2 * tiles, 8, LANES)
     for jh in range(s.cols):
@@ -183,7 +178,7 @@
                 wide_ref[pl.ds(q + r, s.seq, s.block), :] * tw_cols[here, r : r + 1]
             ).astype(BF16)
     load.wait()
-    inner_t = dot(unit(s.n2), inner_ref[...], 1, 1).astype(BF16)
+    inner_t = inner_ref[...].T
     stores = []
     for r in range(s.rows):
         grad = dot(inner_t, col_ref[r], 1, 0)

time: 159 us -> 158 us (level)
  no operation moved by 1% of the time
where the time goes in v8:
time: 158 us; the launch traced here: 157 us
  blocking collectives  131 us (83%)
  Pallas kernels  16 us (10%)
  starting transfers between devices  7.56 us (5%)
  local copies, waits for them, and re-layouts  2 us (1%)
    all_to_all x1, blocking collectives, exchange(): lax.all_to_all(packed, 'seq', split_axis=0, concat_axis=0, tiled=True)  65 us
    all_to_all x1, blocking collectives, on_device(): lax.all_to_all(back_send.reshape(seq * groups, rows, LANES), 'seq', split...  39 us
    pallas_call x5, Pallas kernels, call(): pl.pallas_call(functools.partial(kernel, s), out_shape=[(pltpu.HBM if pla...  16 us
    all_gather x1, blocking collectives, on_device(): sums = lax.all_gather(part_sum, 'chan')  15.8 us
    all_gather x1, blocking collectives, on_device(): projections = lax.all_gather(part_proj, 'chan')  11 us
    all_to_all x1, starting transfers between devices, on_device(): lax.all_to_all(jnp.broadcast_to(share, (seq,) + share.shape), 'seq', spli...  7.56 us
  transfers between devices with their start and end apart: 1, of which 0 were waited for; matrix products, arithmetic and copies ran while one was open for 0% of the time, Pallas kernels for 3%

profile of v8, /device:TPU:1, one launch (start us, length us, event | category | flops | bytes accessed | tf_op | source)
XLA Modules:
  0.0 157.4 jit_solution(5516350896770987247)
XLA Ops:
  0.6 0.0 copy-start
  0.6 1.2 copy-done
  1.9 0.7 squares.1
  2.5 15.8 %all-gather.2.sum_ref = f32[4,4,512]{2,1,0:T(4,128)S(1)} all-gather(f32[1,4,512]{2,1,0:T(4,128)S(1)} %bitcast.15), channel_id=2, replica_groups=mesh['seq'=128,'chan'=4] {'chan'}, dimensions={0}, use_global_device_ids=true | all-gather | bytes 40960 | tf_op jit(solution)/shard_map/all_gather | solution.py:250
  18.3 5.5 %inner.1 = (bf16[8192,128]{1,0:T(8,128)(2,1)S(1)}, f32[4,512]{1,0:T(4,128)S(1)}) custom-call(bf16[4,512,256]{2,1,0:T(8,128)(2,1)} %cot_ref.1, bf16[512,512]{1,0:T(8,128)(2,1)} %inner_hbm.3, bf16[4,512,256]{2,1,0:T(8,128)(2,1)} %x_ref.5, f32[1,256]{1,0:T(1,128)} %bitcast.17, f32[4,512]{1,0:T(4,128)} %tw_ref.1, f32[4,4,512]{2,1,0:T(4,128)S(1)} %all-gather.2.sum_ref), custom_call_target="tpu_custom_call" | custom-call | flops 536870912 | bytes 5242880 | tf_op jit(solution)/shard_map/inner/pallas_call | solution.py:216
  23.8 0.0 copy-start.5
  23.8 0.0 copy-start.6
  23.8 65.0 %all_to_all.15 = bf16[128,64,128]{2,1,0:T(8,128)(2,1)S(1)} all-to-all(bf16[128,64,128]{2,1,0:T(8,128)(2,1)S(1)} %bitcast.12), channel_id=1, replica_groups=mesh['seq'=128,'chan'=4] {'seq'}, dimensions={0} | all-to-all | bytes 4194304 | tf_op jit(solution)/shard_map/all_to_all | solution.py:233
  88.8 0.0 copy-done.5
  88.8 3.3 %middle.1 = bf16[64,2,9,4,128]{4,3,2,1,0:T(4,128)(2,1)S(1)} custom-call(bf16[8192,128]{1,0:T(8,128)(2,1)S(1)} %bitcast.13, bf16[256,256]{1,0:T(8,128)(2,1)S(1)} %bitcast.19, bf16[512,512]{1,0:T(8,128)(2,1)S(1)} %copy-done.5), custom_call_target="tpu_custom_call" | custom-call | flops 1610612736 | bytes 4194304 | tf_op jit(solution)/shard_map/middle/pallas_call | solution.py:216
  92.1 0.0 copy-start.1
  92.1 0.0 copy-start.2
  92.1 0.0 copy-start.3
  92.1 0.0 copy-start.4
  92.1 39.0 %all_to_all.16 = bf16[1152,4,128]{2,1,0:T(4,128)(2,1)S(1)} all-to-all(bf16[1152,4,128]{2,1,0:T(4,128)(2,1)S(1)} %bitcast.14), channel_id=1, replica_groups=mesh['seq'=128,'chan'=4] {'seq'}, dimensions={0} | all-to-all | bytes 2359296 | tf_op jit(solution)/shard_map/all_to_all | solution.py:263
  131.2 0.1 convert_reduce_fusion
  131.3 0.7 broadcast_in_dim.3
  132.1 7.6 %all-to-all-start.2 = ((f32[128,4,128]{2,1,0:T(4,128)}), f32[128,4,128]{2,1,0:T(4,128)}, u32[]{:S(2)}, u32[]{:S(2)}) async-start(f32[128,4,128]{2,1,0:T(4,128)} %broadcast_in_dim.3), calls=%async_computation.2 | async-start | bytes 524288 | tf_op jit(solution)/shard_map/all_to_all | solution.py:267
  139.6 0.0 copy-done.1
  139.6 0.0 copy-done.2
  139.7 4.1 %back.1 = (f32[4,512,256]{2,1,0:T(8,128)}, f32[4,512]{1,0:T(4,128)S(1)}) custom-call(bf16[512,512]{1,0:T(8,128)(2,1)} %inner_hbm.3, bf16[64,2,9,4,128]{4,3,2,1,0:T(4,128)(2,1)S(1)} %bitcast.11, bf16[4,512,256]{2,1,0:T(8,128)(2,1)S(1)} %copy-done.1, bf16[4,512,256]{2,1,0:T(8,128)(2,1)S(1)} %copy-done.2, f32[4,512]{1,0:T(4,128)S(1)} %get-tuple-element.9.inv_ref, ...), custom_call_target="tpu_custom_call" | custom-call | flops 536870912 | bytes 6291456 | tf_op jit(solution)/shard_map/back/pallas_call | solution.py:216
  143.7 11.0 %all-gather.3.proj_ref = f32[4,4,512]{2,1,0:T(4,128)S(1)} all-gather(f32[1,4,512]{2,1,0:T(4,128)S(1)} %bitcast.16), channel_id=3, replica_groups=mesh['seq'=128,'chan'=4] {'chan'}, dimensions={0}, use_global_device_ids=true | all-gather | bytes 40960 | tf_op jit(solution)/shard_map/all_gather | solution.py:275
  154.7 0.0 all-to-all-done.2
  154.7 2.5 %finish.1 = (bf16[4,512,256]{2,1,0:T(8,128)(2,1)}, f32[256,256]{1,0:T(8,128)}) custom-call(f32[4,512,256]{2,1,0:T(8,128)} %get-tuple-element.10.sum_hbm, f32[512,128]{1,0:T(8,128)} %bitcast.7.whole_hbm, bf16[4,512,256]{2,1,0:T(8,128)(2,1)S(1)} %copy-done.1, f32[4,512]{1,0:T(4,128)S(1)} %get-tuple-element.9.inv_ref, f32[4,4,512]{2,1,0:T(4,128)S(1)} %all-gather.3.proj_ref), custom_call_target="tpu_custom_call" | custom-call | flops 5368709 | bytes 4194304 | tf_op jit(solution)/shard_map/finish/pallas_call | solution.py:216
  (3 shorter events, 0.0 us)
Async XLA Ops:
  0.6 1.2 copy-start
  23.8 65.0 %copy-start.5 = (bf16[512,512]{1,0:T(8,128)(2,1)S(1)}, bf16[512,512]{1,0:T(8,128)(2,1)}, u32[]{:S(2)}) copy-start(bf16[512,512]{1,0:T(8,128)(2,1)} %outer_ref.1) | copy-start | bytes 1572868
  23.8 65.0 %copy-start.6 = (bf16[1,256,256]{2,1,0:T(8,128)(2,1)S(1)}, bf16[1,256,256]{2,1,0:T(8,128)(2,1)}, u32[]{:S(2)}) copy-start(bf16[1,256,256]{2,1,0:T(8,128)(2,1)} %param.12) | copy-start | bytes 393220
  92.1 47.5 %copy-start.1 = (bf16[4,512,256]{2,1,0:T(8,128)(2,1)S(1)}, bf16[4,512,256]{2,1,0:T(8,128)(2,1)}, u32[]{:S(2)}) copy-start(bf16[4,512,256]{2,1,0:T(8,128)(2,1)} %x_ref.5) | copy-start | bytes 3145732
  92.1 47.5 %copy-start.2 = (bf16[4,512,256]{2,1,0:T(8,128)(2,1)S(1)}, bf16[4,512,256]{2,1,0:T(8,128)(2,1)}, u32[]{:S(2)}) copy-start(bf16[4,512,256]{2,1,0:T(8,128)(2,1)} %cot_ref.1) | copy-start | bytes 3145732
  92.1 47.5 %copy-start.3 = (f32[4,512]{1,0:T(4,128)S(1)}, f32[4,512]{1,0:T(4,128)}, u32[]{:S(2)}) copy-start(f32[4,512]{1,0:T(4,128)} %tw_ref.1) | copy-start | bytes 24580
  92.1 47.5 %copy-start.4 = (f32[256]{0:T(256)S(1)}, f32[256]{0:T(256)}, u32[]{:S(2)}) copy-start(f32[256]{0:T(256)} %param.8) | copy-start | bytes 3076
  132.1 22.6 %all-to-all-start.2 = ((f32[128,4,128]{2,1,0:T(4,128)}), f32[128,4,128]{2,1,0:T(4,128)}, u32[]{:S(2)}, u32[]{:S(2)}) async-start(f32[128,4,128]{2,1,0:T(4,128)} %broadcast_in_dim.3), calls=%async_computation.2 | async-start | bytes 524288 | tf_op jit(solution)/shard_map/all_to_all | solution.py:267
